TPU v7x, 512 devices: a whole 4x8x8 slice. The times are simulated.
512 devices in a mesh: seg: 32 (over z, x_hi, core), patch: 16 (over x_lo, y).
Axes of the slice: x: 4 (x_hi: 2, x_lo: 2; x = x_hi * 2 + x_lo), y: 8, z: 8, core: 2. Of those that a mesh axis runs over, the one named last changes fastest.
Arguments:
- incident: bfloat16 [32, 64, 4096], P('seg', None, 'patch'), may hold values from -6 to 6
- wall_axial: float32 [32, 4096], P('seg'), may hold values from 0 to 1
- wall_angle: float32 [32, 4096], P('seg'), may hold values from -3.140625 to 3.140625
- wall_area: float32 [32, 4096], P('seg'), may hold values from 0.5 to 2
- visibility: int32 [32, 2, 32, 32], P('seg', None, 'patch'), may hold values 0 or 1
- end_reflection: float32 [2, 32], replicated, may hold values from -0.9 to 0.9
Outputs:
- currents: bfloat16 [32, 64, 4096], P('seg', None, 'patch')
Inputs may be any that keep to these rules, and one draw needn't show every extreme that they name: `visibility`: 1 where the source block is lit for the target block, 0 where it is in shadow.
All inputs are finite; a program needn't handle non-finite values.
Results may differ from a plain program's by a relative error of at most 0.0034.
Values may be sent and summed in bfloat16 or wider, within the bound.
A program may use at most 64 MiB of HBM per device.

v0:
```python
import math

import jax
import jax.numpy as jnp
from jax import lax
from jax.sharding import PartitionSpec as P

ITERS = 2


WAVENUMBER = 40.0
RADIUS = 0.5
SOFTENING = 0.25


def extended(x, sides, width):
    for axis, dim in sides:
        count, length = (lax.axis_size(axis), x.shape[dim])
        up = [(i, (i + 1) % count) for i in range(count - 1)]
        down = [(j, i) for i, j in up]
        last = lax.slice_in_dim(x, length - width, length, axis=dim)
        leading = lax.slice_in_dim(x, 0, width, axis=dim)
        before = lax.ppermute(last, axis, up)
        after = lax.ppermute(leading, axis, down)
        x = jnp.concatenate([before, x, after], axis=dim)
    return x


def from_behind(value, axis, steps):
    count = lax.axis_size(axis)
    leading, last = (max(0, -steps), min(count, count - steps))
    return lax.ppermute(value, axis, [(source, source + steps) for source in range(leading, last)])


def from_everyone(x, axis):
    copies = jnp.broadcast_to(x, (lax.axis_size(axis), *x.shape))
    return lax.all_to_all(copies, axis, split_axis=0, concat_axis=0, tiled=True)


def in_order(blocks, dim):
    blocks = jnp.moveaxis(blocks, 0, dim)
    lengths = blocks.shape
    return blocks.reshape(*lengths[:dim], lengths[dim] * lengths[dim + 1], *lengths[dim + 2 :])


def gather_directly(x, axis, dim):
    blocks = from_everyone(x, axis)
    return in_order(blocks, dim)


def in_one_piece(arrays, axis, dim, along):
    widths = [a.shape[along] for a in arrays]
    both = jnp.concatenate(arrays, axis=along)
    result = gather_directly(both, axis, dim)
    return tuple(jnp.split(result, [sum(widths[:k]) for k in range(1, len(widths))], axis=along))


def kernel_piece(target, source, offset, visible, patches):
    axial_gap = offset + target[0][:, None] - source[0][None, :]
    chord = 2.0 * RADIUS * RADIUS * (1.0 - jnp.cos(target[1][:, None] - source[1][None, :]))
    squared = axial_gap * axial_gap + chord
    magnitude = (
        source[2][None, :] * visible.astype(jnp.float32) / jnp.sqrt(patches * (squared + SOFTENING))
    )
    phases = WAVENUMBER * jnp.sqrt(squared)
    kernel_re = (magnitude * jnp.cos(phases)).astype(jnp.bfloat16)
    kernel_im = (-magnitude * jnp.sin(phases)).astype(jnp.bfloat16)
    return (kernel_re, kernel_im)


def couple(sources, kernel_re, kernel_im, angles):
    contract = (((1,), (1,)), ((), ()))
    prod_re = lax.dot_general(sources, kernel_re, contract, preferred_element_type=jnp.float32)
    prod_im = lax.dot_general(sources, kernel_im, contract, preferred_element_type=jnp.float32)
    return jnp.concatenate(
        [prod_re[:angles] - prod_im[angles:], prod_re[angles:] + prod_im[:angles]], 0
    )


def reflect(coef, values, angles):
    coef_re = coef[:angles][:, None]
    coef_im = coef[angles:][:, None]
    real_part = values[:angles]
    imag_part = values[angles:]
    return jnp.concatenate(
        [coef_re * real_part - coef_im * imag_part, coef_re * imag_part + coef_im * real_part], 0
    )


def on_device(incident, wall_axial, wall_angle, wall_area, visibility, end_reflection):
    channel_count = incident.shape[1]
    target_rows = incident.shape[2]
    patches = wall_axial.shape[1]
    angles = channel_count // 4
    block_size = patches // visibility.shape[3]
    seg_count = lax.axis_size("seg")
    seg_index = lax.axis_index("seg")
    patch_index = lax.axis_index("patch")
    geometry = jnp.stack([wall_axial[0], wall_angle[0], wall_area[0]])[None]
    nearby = extended(geometry, (("seg", 0),), 1)
    before_geo = nearby[0]
    after_geo = nearby[2]
    target = lax.dynamic_slice_in_dim(geometry[0], patch_index * target_rows, target_rows, 1)
    lit_rows = jnp.repeat(visibility[0], block_size, axis=1)
    gen_rows = math.gcd(32, target_rows)

    def build_block(block_index):
        row_start = block_index * gen_rows
        target_block = lax.dynamic_slice_in_dim(target, row_start, gen_rows, 1)
        lit_block = lax.dynamic_slice_in_dim(lit_rows, row_start, gen_rows, 1)
        lit_block = jnp.repeat(lit_block, block_size, axis=2)
        fore_re, fore_im = kernel_piece(target_block, before_geo, 1.0, lit_block[0], patches)
        back_re, back_im = kernel_piece(target_block, after_geo, -1.0, lit_block[1], patches)
        return (fore_re, fore_im, back_re, back_im)

    tables = lax.map(build_block, jnp.arange(target_rows // gen_rows, dtype=jnp.int32))
    fore_re, fore_im, back_re, back_im = [table.reshape(target_rows, patches) for table in tables]
    at_first = seg_index == 0
    at_last = seg_index == seg_count - 1
    state = incident
    for sweep in range(ITERS):
        before_cur = from_behind(state[0, : 2 * angles], "seg", 1)
        after_cur = from_behind(state[0, 2 * angles :], "seg", -1)
        pieces = in_one_piece((before_cur, after_cur), "patch", 1, 0)
        forward = couple(pieces[0], fore_re, fore_im, angles)
        backward = couple(pieces[1], back_re, back_im, angles)
        coupled = jnp.concatenate([forward, backward], 0)
        previous = state[0].astype(jnp.float32)
        first_end = reflect(end_reflection[0], previous[2 * angles :], angles)
        last_end = reflect(end_reflection[1], previous[: 2 * angles], angles)
        mirrored = jnp.concatenate(
            [jnp.where(at_first, first_end, 0.0), jnp.where(at_last, last_end, 0.0)], 0
        )
        state = (incident[0].astype(jnp.float32) + coupled + mirrored).astype(jnp.bfloat16)[None]
    return state


def solution(mesh):
    return jax.shard_map(
        on_device,
        mesh=mesh,
        in_specs=(
            P("seg", None, "patch"),
            P("seg", None),
            P("seg", None),
            P("seg", None),
            P("seg", None, "patch", None),
            P(),
        ),
        out_specs=P("seg", None, "patch"),
        check_vma=False,
    )
```

profile of v0, /device:TPU:207, one launch (start us, length us, event | category | flops | bytes accessed | tf_op | source)
XLA Modules:
  0.0 164.4 jit_solution(8647552586597011998)
XLA Ops:
  0.8 6.6 %collective-permute-start.2 = (f32[1,3,4096]{2,1,0:T(4,128)S(1)}, f32[1,3,4096]{2,1,0:T(4,128)S(1)}, u32[]{:S(2)}, u32[]{:S(2)}) collective-permute-start(f32[1,3,4096]{2,1,0:T(4,128)S(1)} %get-tuple-element.129), channel_id=1, source_target_pairs={{0,16},{16,32},{32,48},{48,64},{64,80},{80,96},{96,112},{112,128},... | collective-permute-start | bytes 147464 | tf_op jit(solution)/shard_map/ppermute | solution.py:23
  7.4 1.9 %collective-permute-start.3 = (f32[1,3,4096]{2,1,0:T(4,128)S(1)}, f32[1,3,4096]{2,1,0:T(4,128)S(1)}, u32[]{:S(2)}, u32[]{:S(2)}) collective-permute-start(f32[1,3,4096]{2,1,0:T(4,128)S(1)} %get-tuple-element.129), channel_id=1, source_target_pairs={{16,0},{32,16},{48,32},{64,48},{80,64},{96,80},{112,96},{128,112},... | collective-permute-start | bytes 147464 | tf_op jit(solution)/shard_map/ppermute | solution.py:24
  10.1 7.2 %collective-permute-start = (bf16[32,256]{1,0:T(8,128)(2,1)S(1)}, bf16[32,256]{1,0:T(8,128)(2,1)S(1)}, u32[]{:S(2)}, u32[]{:S(2)}) collective-permute-start(bf16[32,256]{1,0:T(8,128)(2,1)S(1)} %get-tuple-element.132), channel_id=1, source_target_pairs={{0,16},{16,32},{32,48},{48,64},{64,80},{80,96},{96,112},{112,128},... | collective-permute-start | bytes 49160 | tf_op jit(solution)/shard_map/ppermute | solution.py:32
  17.4 1.9 %collective-permute-start.1 = (bf16[32,256]{1,0:T(8,128)(2,1)S(1)}, bf16[32,256]{1,0:T(8,128)(2,1)S(1)}, u32[]{:S(2)}, u32[]{:S(2)}) collective-permute-start(bf16[32,256]{1,0:T(8,128)(2,1)S(1)} %get-tuple-element.133), channel_id=1, source_target_pairs={{16,0},{32,16},{48,32},{64,48},{80,64},{96,80},{112,96},{128,112},... | collective-permute-start | bytes 49160 | tf_op jit(solution)/shard_map/ppermute | solution.py:32
  20.1 0.9 slice_bitcast_fusion.16
  21.1 4.9 %collective-permute-done.1 = bf16[32,256]{1,0:T(8,128)(2,1)S(1)} collective-permute-done((bf16[32,256]{1,0:T(8,128)(2,1)S(1)}, bf16[32,256]{1,0:T(8,128)(2,1)S(1)}, u32[]{:S(2)}, u32[]{:S(2)}) %collective-permute-start.1) | collective-permute-done | bytes 16416 | tf_op jit(solution)/shard_map/ppermute | solution.py:32
  26.0 0.9 broadcast_in_dim.41
  26.9 7.9 %all-to-all-start = ((bf16[16,64,256]{2,1,0:T(8,128)(2,1)}), bf16[16,64,256]{2,1,0:T(8,128)(2,1)S(1)}, u32[]{:S(2)}, u32[]{:S(2)}) async-start(bf16[16,64,256]{2,1,0:T(8,128)(2,1)} %broadcast_in_dim.41), calls=%async_computation | async-start | bytes 1048576 | tf_op jit(solution)/shard_map/all_to_all | solution.py:37
  34.9 88.4 %while.16 = (s32[]{:T(128)}, bf16[8,32,4096]{2,1,0:T(8,128)(2,1)}, bf16[8,32,4096]{2,1,0:T(8,128)(2,1)}, bf16[8,32,4096]{2,1,0:T(8,128)(2,1)}, bf16[8,32,4096]{2...) while((s32[]{:T(128)}, bf16[8,32,4096]{2,1,0:T(8,128)(2,1)}, ...), condition=%wide.region_1.2_spmd, body=%wide.region_0.1_spmd.sunk | while | flops 4196423 | bytes 5564895 | solution.py:116
  36.9 9.1 %fusion.49 = (bf16[8,32,4096]{2,1,0:T(8,128)(2,1)}, bf16[8,32,4096]{2,1,0:T(8,128)(2,1)}, bf16[8,32,4096]{2,1,0:T(8,128)(2,1)}, bf16[8,32,4096]{2,1,0:T(8,128)(2,1)}) fusion(bf16[8,32,4096]{2,1,0:T(8,128)(2,1)} %get-tuple-element.254, s32[]{:T(128)} %get-tuple-element.250, f32[4096]{0:T(1024)S(1)} %bitcast.165, f32[4096]{0:T(1024)S(1)} %bitcast.166, ...), kind=kLoop, calls=%fused_computation.13.clone.1 | loop fusion | flops 4194304 | bytes 2196352 | tf_op jit(solution)/shard_map/while/body/jit(dynamic_update_index_in_dim)/dynamic_update_slice | solution.py:116
  48.0 9.0 %fusion.49 = (bf16[8,32,4096]{2,1,0:T(8,128)(2,1)}, bf16[8,32,4096]{2,1,0:T(8,128)(2,1)}, bf16[8,32,4096]{2,1,0:T(8,128)(2,1)}, bf16[8,32,4096]{2,1,0:T(8,128)(2,1)}) fusion(bf16[8,32,4096]{2,1,0:T(8,128)(2,1)} %get-tuple-element.254, s32[]{:T(128)} %get-tuple-element.250, f32[4096]{0:T(1024)S(1)} %bitcast.165, f32[4096]{0:T(1024)S(1)} %bitcast.166, ...), kind=kLoop, calls=%fused_computation.13.clone.1 | loop fusion | flops 4194304 | bytes 2196352 | tf_op jit(solution)/shard_map/while/body/jit(dynamic_update_index_in_dim)/dynamic_update_slice | solution.py:116
  59.0 9.1 %fusion.49 = (bf16[8,32,4096]{2,1,0:T(8,128)(2,1)}, bf16[8,32,4096]{2,1,0:T(8,128)(2,1)}, bf16[8,32,4096]{2,1,0:T(8,128)(2,1)}, bf16[8,32,4096]{2,1,0:T(8,128)(2,1)}) fusion(bf16[8,32,4096]{2,1,0:T(8,128)(2,1)} %get-tuple-element.254, s32[]{:T(128)} %get-tuple-element.250, f32[4096]{0:T(1024)S(1)} %bitcast.165, f32[4096]{0:T(1024)S(1)} %bitcast.166, ...), kind=kLoop, calls=%fused_computation.13.clone.1 | loop fusion | flops 4194304 | bytes 2196352 | tf_op jit(solution)/shard_map/while/body/jit(dynamic_update_index_in_dim)/dynamic_update_slice | solution.py:116
  70.1 9.0 %fusion.49 = (bf16[8,32,4096]{2,1,0:T(8,128)(2,1)}, bf16[8,32,4096]{2,1,0:T(8,128)(2,1)}, bf16[8,32,4096]{2,1,0:T(8,128)(2,1)}, bf16[8,32,4096]{2,1,0:T(8,128)(2,1)}) fusion(bf16[8,32,4096]{2,1,0:T(8,128)(2,1)} %get-tuple-element.254, s32[]{:T(128)} %get-tuple-element.250, f32[4096]{0:T(1024)S(1)} %bitcast.165, f32[4096]{0:T(1024)S(1)} %bitcast.166, ...), kind=kLoop, calls=%fused_computation.13.clone.1 | loop fusion | flops 4194304 | bytes 2196352 | tf_op jit(solution)/shard_map/while/body/jit(dynamic_update_index_in_dim)/dynamic_update_slice | solution.py:116
  81.1 9.1 %fusion.49 = (bf16[8,32,4096]{2,1,0:T(8,128)(2,1)}, bf16[8,32,4096]{2,1,0:T(8,128)(2,1)}, bf16[8,32,4096]{2,1,0:T(8,128)(2,1)}, bf16[8,32,4096]{2,1,0:T(8,128)(2,1)}) fusion(bf16[8,32,4096]{2,1,0:T(8,128)(2,1)} %get-tuple-element.254, s32[]{:T(128)} %get-tuple-element.250, f32[4096]{0:T(1024)S(1)} %bitcast.165, f32[4096]{0:T(1024)S(1)} %bitcast.166, ...), kind=kLoop, calls=%fused_computation.13.clone.1 | loop fusion | flops 4194304 | bytes 2196352 | tf_op jit(solution)/shard_map/while/body/jit(dynamic_update_index_in_dim)/dynamic_update_slice | solution.py:116
  92.2 9.0 %fusion.49 = (bf16[8,32,4096]{2,1,0:T(8,128)(2,1)}, bf16[8,32,4096]{2,1,0:T(8,128)(2,1)}, bf16[8,32,4096]{2,1,0:T(8,128)(2,1)}, bf16[8,32,4096]{2,1,0:T(8,128)(2,1)}) fusion(bf16[8,32,4096]{2,1,0:T(8,128)(2,1)} %get-tuple-element.254, s32[]{:T(128)} %get-tuple-element.250, f32[4096]{0:T(1024)S(1)} %bitcast.165, f32[4096]{0:T(1024)S(1)} %bitcast.166, ...), kind=kLoop, calls=%fused_computation.13.clone.1 | loop fusion | flops 4194304 | bytes 2196352 | tf_op jit(solution)/shard_map/while/body/jit(dynamic_update_index_in_dim)/dynamic_update_slice | solution.py:116
  103.3 9.0 %fusion.49 = (bf16[8,32,4096]{2,1,0:T(8,128)(2,1)}, bf16[8,32,4096]{2,1,0:T(8,128)(2,1)}, bf16[8,32,4096]{2,1,0:T(8,128)(2,1)}, bf16[8,32,4096]{2,1,0:T(8,128)(2,1)}) fusion(bf16[8,32,4096]{2,1,0:T(8,128)(2,1)} %get-tuple-element.254, s32[]{:T(128)} %get-tuple-element.250, f32[4096]{0:T(1024)S(1)} %bitcast.165, f32[4096]{0:T(1024)S(1)} %bitcast.166, ...), kind=kLoop, calls=%fused_computation.13.clone.1 | loop fusion | flops 4194304 | bytes 2196352 | tf_op jit(solution)/shard_map/while/body/jit(dynamic_update_index_in_dim)/dynamic_update_slice | solution.py:116
  114.3 9.0 %fusion.49 = (bf16[8,32,4096]{2,1,0:T(8,128)(2,1)}, bf16[8,32,4096]{2,1,0:T(8,128)(2,1)}, bf16[8,32,4096]{2,1,0:T(8,128)(2,1)}, bf16[8,32,4096]{2,1,0:T(8,128)(2,1)}) fusion(bf16[8,32,4096]{2,1,0:T(8,128)(2,1)} %get-tuple-element.254, s32[]{:T(128)} %get-tuple-element.250, f32[4096]{0:T(1024)S(1)} %bitcast.165, f32[4096]{0:T(1024)S(1)} %bitcast.166, ...), kind=kLoop, calls=%fused_computation.13.clone.1 | loop fusion | flops 4194304 | bytes 2196352 | tf_op jit(solution)/shard_map/while/body/jit(dynamic_update_index_in_dim)/dynamic_update_slice | solution.py:116
  123.4 2.5 %fusion.20 = f32[32,256]{1,0:T(8,128)S(1)} fusion(bf16[32,4096]{1,0:T(8,128)(2,1)S(1)} %bitcast.157, bf16[256,4096]{1,0:T(8,128)(2,1)} %bitcast.143), kind=kOutput, calls=%fused_computation.81 | convolution fusion | flops 67108864 | bytes 2392064 | tf_op jit(solution)/shard_map/dot_general | solution.py:73
  128.4 3.1 %collective-permute-start.4 = (bf16[32,256]{1,0:T(8,128)(2,1)S(1)}, bf16[32,256]{1,0:T(8,128)(2,1)S(1)}, u32[]{:S(2)}, u32[]{:S(2)}) collective-permute-start(bf16[32,256]{1,0:T(8,128)(2,1)S(1)} %get-tuple-element.130), channel_id=1, source_target_pairs={{0,16},{16,32},{32,48},{48,64},{64,80},{80,96},{96,112},{112,128},... | collective-permute-start | bytes 49160 | tf_op jit(solution)/shard_map/ppermute | solution.py:32
  131.5 1.9 %collective-permute-start.5 = (bf16[32,256]{1,0:T(8,128)(2,1)S(1)}, bf16[32,256]{1,0:T(8,128)(2,1)S(1)}, u32[]{:S(2)}, u32[]{:S(2)}) collective-permute-start(bf16[32,256]{1,0:T(8,128)(2,1)S(1)} %get-tuple-element.131), channel_id=1, source_target_pairs={{16,0},{32,16},{48,32},{64,48},{80,64},{96,80},{112,96},{128,112},... | collective-permute-start | bytes 49160 | tf_op jit(solution)/shard_map/ppermute | solution.py:32
  133.4 6.7 %collective-permute-done.5 = bf16[32,256]{1,0:T(8,128)(2,1)S(1)} collective-permute-done((bf16[32,256]{1,0:T(8,128)(2,1)S(1)}, bf16[32,256]{1,0:T(8,128)(2,1)S(1)}, u32[]{:S(2)}, u32[]{:S(2)}) %collective-permute-start.5) | collective-permute-done | bytes 16416 | tf_op jit(solution)/shard_map/ppermute | solution.py:32
  140.1 0.9 broadcast_in_dim.45
  141.0 7.6 %all-to-all-start.1 = ((bf16[16,64,256]{2,1,0:T(8,128)(2,1)}), bf16[16,64,256]{2,1,0:T(8,128)(2,1)S(1)}, u32[]{:S(2)}, u32[]{:S(2)}) async-start(bf16[16,64,256]{2,1,0:T(8,128)(2,1)} %broadcast_in_dim.45), calls=%async_computation.1 | async-start | bytes 1048576 | tf_op jit(solution)/shard_map/all_to_all | solution.py:37
  148.7 10.9 %all-to-all-done.1 = bf16[16,64,256]{2,1,0:T(8,128)(2,1)S(1)} async-done(((bf16[16,64,256]{2,1,0:T(8,128)(2,1)}), bf16[16,64,256]{2,1,0:T(8,128)(2,1)S(1)}, u32[]{:S(2)}, u32[]{:S(2)}) %all-to-all-start.1) | async-done | bytes 524320 | tf_op jit(solution)/shard_map/all_to_all | solution.py:37
  (133 shorter events, 20.4 us)
Async XLA Ops:
  0.0 34.9 %copy-start.8 = (s32[1,2,2,32]{3,2,1,0:T(2,128)S(1)}, s32[1,2,2,32]{3,2,1,0:T(2,128)}, u32[]{:S(2)}) copy-start(s32[1,2,2,32]{3,2,1,0:T(2,128)} %param.12) | copy-start | bytes 1540
  0.8 34.0 %collective-permute-start.2 = (f32[1,3,4096]{2,1,0:T(4,128)S(1)}, f32[1,3,4096]{2,1,0:T(4,128)S(1)}, u32[]{:S(2)}, u32[]{:S(2)}) collective-permute-start(f32[1,3,4096]{2,1,0:T(4,128)S(1)} %get-tuple-element.129), channel_id=1, source_target_pairs={{0,16},{16,32},{32,48},{48,64},{64,80},{80,96},{96,112},{112,128},... | collective-permute-start | bytes 147464 | tf_op jit(solution)/shard_map/ppermute | solution.py:23
  7.4 27.4 %collective-permute-start.3 = (f32[1,3,4096]{2,1,0:T(4,128)S(1)}, f32[1,3,4096]{2,1,0:T(4,128)S(1)}, u32[]{:S(2)}, u32[]{:S(2)}) collective-permute-start(f32[1,3,4096]{2,1,0:T(4,128)S(1)} %get-tuple-element.129), channel_id=1, source_target_pairs={{16,0},{32,16},{48,32},{64,48},{80,64},{96,80},{112,96},{128,112},... | collective-permute-start | bytes 147464 | tf_op jit(solution)/shard_map/ppermute | solution.py:24
  10.1 11.0 %collective-permute-start = (bf16[32,256]{1,0:T(8,128)(2,1)S(1)}, bf16[32,256]{1,0:T(8,128)(2,1)S(1)}, u32[]{:S(2)}, u32[]{:S(2)}) collective-permute-start(bf16[32,256]{1,0:T(8,128)(2,1)S(1)} %get-tuple-element.132), channel_id=1, source_target_pairs={{0,16},{16,32},{32,48},{48,64},{64,80},{80,96},{96,112},{112,128},... | collective-permute-start | bytes 49160 | tf_op jit(solution)/shard_map/ppermute | solution.py:32
  17.4 8.7 %collective-permute-start.1 = (bf16[32,256]{1,0:T(8,128)(2,1)S(1)}, bf16[32,256]{1,0:T(8,128)(2,1)S(1)}, u32[]{:S(2)}, u32[]{:S(2)}) collective-permute-start(bf16[32,256]{1,0:T(8,128)(2,1)S(1)} %get-tuple-element.133), channel_id=1, source_target_pairs={{16,0},{32,16},{48,32},{64,48},{80,64},{96,80},{112,96},{128,112},... | collective-permute-start | bytes 49160 | tf_op jit(solution)/shard_map/ppermute | solution.py:32
  26.9 96.4 %all-to-all-start = ((bf16[16,64,256]{2,1,0:T(8,128)(2,1)}), bf16[16,64,256]{2,1,0:T(8,128)(2,1)S(1)}, u32[]{:S(2)}, u32[]{:S(2)}) async-start(bf16[16,64,256]{2,1,0:T(8,128)(2,1)} %broadcast_in_dim.41), calls=%async_computation | async-start | bytes 1048576 | tf_op jit(solution)/shard_map/all_to_all | solution.py:37
  123.3 2.6 %copy-start.1 = (bf16[8,32,4096]{2,1,0:T(8,128)(2,1)S(1)}, bf16[8,32,4096]{2,1,0:T(8,128)(2,1)}, u32[]{:S(2)}) copy-start(bf16[8,32,4096]{2,1,0:T(8,128)(2,1)} %get-tuple-element.61) | copy-start | bytes 6291460
  123.4 3.3 %copy-start.3 = (bf16[8,32,4096]{2,1,0:T(8,128)(2,1)S(1)}, bf16[8,32,4096]{2,1,0:T(8,128)(2,1)}, u32[]{:S(2)}) copy-start(bf16[8,32,4096]{2,1,0:T(8,128)(2,1)} %get-tuple-element.62) | copy-start | bytes 6291460
  125.9 1.7 %copy-start.5 = (bf16[8,32,4096]{2,1,0:T(8,128)(2,1)S(1)}, bf16[8,32,4096]{2,1,0:T(8,128)(2,1)}, u32[]{:S(2)}) copy-start(bf16[8,32,4096]{2,1,0:T(8,128)(2,1)} %get-tuple-element.63) | copy-start | bytes 6291460
  126.7 1.6 %copy-start.7 = (bf16[1,64,256]{2,1,0:T(8,128)(2,1)S(1)}, bf16[1,64,256]{2,1,0:T(8,128)(2,1)}, u32[]{:S(2)}) copy-start(bf16[1,64,256]{2,1,0:T(8,128)(2,1)} %param.8) | copy-start | bytes 98308
  128.3 31.4 %copy-start = (bf16[8,32,4096]{2,1,0:T(8,128)(2,1)S(1)}, bf16[8,32,4096]{2,1,0:T(8,128)(2,1)}, u32[]{:S(2)}) copy-start(bf16[8,32,4096]{2,1,0:T(8,128)(2,1)} %get-tuple-element.60) | copy-start | bytes 6291460
  128.4 5.0 %collective-permute-start.4 = (bf16[32,256]{1,0:T(8,128)(2,1)S(1)}, bf16[32,256]{1,0:T(8,128)(2,1)S(1)}, u32[]{:S(2)}, u32[]{:S(2)}) collective-permute-start(bf16[32,256]{1,0:T(8,128)(2,1)S(1)} %get-tuple-element.130), channel_id=1, source_target_pairs={{0,16},{16,32},{32,48},{48,64},{64,80},{80,96},{96,112},{112,128},... | collective-permute-start | bytes 49160 | tf_op jit(solution)/shard_map/ppermute | solution.py:32
  131.5 8.7 %collective-permute-start.5 = (bf16[32,256]{1,0:T(8,128)(2,1)S(1)}, bf16[32,256]{1,0:T(8,128)(2,1)S(1)}, u32[]{:S(2)}, u32[]{:S(2)}) collective-permute-start(bf16[32,256]{1,0:T(8,128)(2,1)S(1)} %get-tuple-element.131), channel_id=1, source_target_pairs={{16,0},{32,16},{48,32},{64,48},{80,64},{96,80},{112,96},{128,112},... | collective-permute-start | bytes 49160 | tf_op jit(solution)/shard_map/ppermute | solution.py:32
  141.0 18.7 %all-to-all-start.1 = ((bf16[16,64,256]{2,1,0:T(8,128)(2,1)}), bf16[16,64,256]{2,1,0:T(8,128)(2,1)S(1)}, u32[]{:S(2)}, u32[]{:S(2)}) async-start(bf16[16,64,256]{2,1,0:T(8,128)(2,1)} %broadcast_in_dim.45), calls=%async_computation.1 | async-start | bytes 1048576 | tf_op jit(solution)/shard_map/all_to_all | solution.py:37
  159.7 1.6 copy-start.2
  159.8 2.3 %copy-start.4 = (bf16[8,32,4096]{2,1,0:T(8,128)(2,1)S(1)}, bf16[8,32,4096]{2,1,0:T(8,128)(2,1)}, u32[]{:S(2)}) copy-start(bf16[8,32,4096]{2,1,0:T(8,128)(2,1)} %get-tuple-element.62) | copy-start | bytes 6291460
  161.3 1.7 %copy-start.6 = (bf16[8,32,4096]{2,1,0:T(8,128)(2,1)S(1)}, bf16[8,32,4096]{2,1,0:T(8,128)(2,1)}, u32[]{:S(2)}) copy-start(bf16[8,32,4096]{2,1,0:T(8,128)(2,1)} %get-tuple-element.63) | copy-start | bytes 6291460
where the time goes:
time: 165 us; the launch traced here: 164 us
  other arithmetic  74.9 us (45%)
  starting transfers between devices  38.1 us (23%)
  waiting for transfers between devices  22.6 us (14%)
  local copies, waits for them, and re-layouts  15.4 us (9%)
  matrix products  7.52 us (5%)
  loops' own time  5.42 us (3%)
    dynamic_update_slice x8, other arithmetic, on_device(): lax.map(build_block, jnp.arange(target_rows // gen_rows, dtype=jnp.int32))  72.4 us
    all_to_all x2, starting transfers between devices, from_everyone(): return lax.all_to_all(copies, axis, split_axis=0, concat_axis=0, tiled=True)  15.5 us
    ppermute x4, starting transfers between devices, from_behind(): lax.ppermute(value, axis, [(source, source + steps) for source in range(l...  14.1 us
    ppermute x4, waiting for transfers between devices, from_behind(): lax.ppermute(value, axis, [(source, source + steps) for source in range(l...  11.6 us
    all_to_all x2, waiting for transfers between devices, from_everyone(): return lax.all_to_all(copies, axis, split_axis=0, concat_axis=0, tiled=True)  11 us
    ppermute x1, starting transfers between devices, extended(): before = lax.ppermute(last, axis, up)  6.61 us
    another operation x1, loops' own time, on_device(): lax.map(build_block, jnp.arange(target_rows // gen_rows, dtype=jnp.int32))  5.42 us
    dynamic_slice x8, local copies, waits for them, and re-layouts, on_device(): lax.map(build_block, jnp.arange(target_rows // gen_rows, dtype=jnp.int32))  4.75 us
  transfers between devices with their start and end apart: 8, of which 3 were waited for; matrix products, arithmetic and copies ran while one was open for 53% of the time, Pallas kernels for 0%

commit v1 on v0

v1 whole, which is shorter than its diff:
```python
import functools
import math

import jax
import jax.numpy as jnp
from jax import lax
from jax.experimental import pallas as pl
from jax.experimental.pallas import tpu as pltpu
from jax.sharding import PartitionSpec as P

ITERS = 2
WAVENUMBER = 40.0
RADIUS = 0.5
SOFTENING = 0.25

MESH = pl.DeviceIdType.MESH
f32, bf16 = jnp.float32, jnp.bfloat16
NT = (((1,), (1,)), ((), ()))

KAPPA = WAVENUMBER / (2.0 * math.pi)
KAPPA2 = KAPPA * KAPPA
CHORD = 2.0 * RADIUS * RADIUS * KAPPA2
ROOT_CHORD = math.sqrt(CHORD)
MAGIC = 12582912.0
DARK = 2.0**127
SIN = (4.441535736857015, -7.264681196614785, 3.252051034939137)
COS = (1.4142040822010087, -6.977642112452626, 5.715238841259401, -1.728349684464805)
TURN = (
    6.283185306487509,
    -41.341701929774175,
    81.60520943123053,
    -76.70366783378654,
    41.999989934944594,
    -14.337025371611837,
)
TILE = 256
ROWS = 32
GROUPS = 6


def poly(x, coefs):
    total = coefs[-1]
    for c in coefs[-2::-1]:
        total = c + x * total
    return total


def split3(x):
    hi = x.astype(bf16).astype(f32)
    rest = x - hi
    mid = rest.astype(bf16).astype(f32)
    return hi, mid, rest - mid


def trig_rows(angle, row):
    g = angle * (0.5 / math.pi) + jnp.where(row == 3, 0.25, 0.0)
    g = jnp.where(g > 0.5, g - 1.0, g)
    h = jnp.where(g > 0.25, 0.5 - g, jnp.where(g < -0.25, -0.5 - g, g))
    return h * poly(h * h, TURN)


def target_features(axial, angle, into, d):
    width = axial.shape[1]
    row = lax.broadcasted_iota(jnp.int32, (8, width), 0)
    lane = lax.broadcasted_iota(jnp.int32, (8, width), 1)
    a = KAPPA * (axial if d == 0 else 1.0 - axial)
    q = jnp.where(row == 0, a * a, jnp.where(row == 1, a, 1.0))
    q = jnp.where(row >= 3, ROOT_CHORD * trig_rows(angle, row), q)
    block = jnp.where(lane < width // 2, 5, 6)
    q = jnp.where(row >= 5, jnp.where(row == block, 2.0, 0.0), q)
    hi, mid, low = split3(q)
    full = jnp.concatenate([hi, hi, hi, mid, mid, low], 0)
    full = jnp.concatenate([full, jnp.zeros((128 - 8 * GROUPS, width), f32)], 0)
    into[d] = full.T[:, : 8 * GROUPS].astype(bf16)


def source_features(geo, lit, into, d, patches):
    row = lax.broadcasted_iota(jnp.int32, (8, 128), 0)

    def block(jb, _):
        sl = pl.ds(pl.multiple_of(jb * 128, 128), 128)
        axial = jnp.broadcast_to(geo[d, 0, :, sl], (8, 128))
        angle = jnp.broadcast_to(geo[d, 1, :, sl], (8, 128))
        area = jnp.broadcast_to(geo[d, 2, :, sl], (8, 128))
        b = KAPPA * jnp.where(d == 0, 1.0 - axial, axial)
        bb = b * b + CHORD
        low_rows = jnp.where(row == 0, 1.0, jnp.where(row == 1, 2.0 * b, bb))
        trig = jnp.where(row >= 5, 0.0, -ROOT_CHORD * trig_rows(angle, row))
        q = jnp.where(row >= 3, trig, low_rows)
        weight = (patches / KAPPA2) / (area * area)
        soft = jnp.where(row == 2, q + SOFTENING * KAPPA2, q) * weight
        dark0 = (1 - lit[0, d, 0, jb]).astype(f32) * DARK
        dark1 = (1 - lit[0, d, 1, jb]).astype(f32) * DARK
        soft = jnp.where(row == 5, dark0, jnp.where(row == 6, dark1, soft))
        for which, value in ((0, q), (1, soft)):
            hi, mid, low = split3(value)
            into[d, which, :, sl] = jnp.concatenate([hi, mid, low, hi, mid, hi], 0).astype(bf16)
        return 0

    lax.fori_loop(0, patches // 128, block, 0, unroll=4)


def kernel_tile(q_ref, soft_ref, table, at):
    for i0 in range(0, TILE, ROWS):
        sl = pl.ds(i0, ROWS)
        q = jnp.maximum(q_ref[sl, :], 1e-30)
        m = lax.rsqrt(soft_ref[sl, :])
        t = q * lax.rsqrt(q)
        f = t - ((t + MAGIC) - MAGIC)
        ff = f * f
        s = f * poly(ff, SIN)
        c = poly(ff, COS)
        u = m * s
        table[at, sl, 0:TILE] = (m - u * s).astype(bf16)
        table[at, sl, TILE : 2 * TILE] = (u * c).astype(bf16)


def build_tables(d, tfeat, sfeat, buffers, tables, tiles):
    def distances(tile, pair):
        js = pl.ds(pl.multiple_of(tile * TILE, TILE), TILE)
        for which in (0, 1):
            pair[which][...] = jnp.dot(
                tfeat[d], sfeat[d, which, :, js], preferred_element_type=f32
            )

    distances(0, buffers[0])

    def step(k, _):
        distances(2 * k + 1, buffers[1])
        kernel_tile(*buffers[0], tables[0], d * (tiles // 2) + k)
        distances(jnp.minimum(2 * k + 2, tiles - 1), buffers[0])
        kernel_tile(*buffers[1], tables[1], d * (tiles // 2) + k)
        return 0

    lax.fori_loop(0, tiles // 2, step, 0)


def couple(d, blocks, tables, tiles, half):
    def product(tile, k, par):
        c = blocks[d, 2 * k + par]
        turned = jnp.concatenate([c[half:], -c[:half]], 0)
        both = jnp.concatenate([c, turned], 1)
        return lax.dot_general(both, tables[par][tile], NT, preferred_element_type=f32)

    def step(k, total):
        tile = d * (tiles // 2) + k
        return total + product(tile, k, 0) + product(tile, k, 1)

    return lax.fori_loop(0, tiles // 2, step, jnp.zeros((2 * half, TILE), f32), unroll=8)


def column(row_values, start, count):
    row = lax.broadcasted_iota(jnp.int32, (count, row_values.shape[1]), 0)
    lane = lax.broadcasted_iota(jnp.int32, (count, row_values.shape[1]), 1)
    wide = jnp.broadcast_to(row_values, (count, row_values.shape[1]))
    return jnp.sum(jnp.where(lane == row + start, wide, 0.0), axis=1, keepdims=True)


def reflect(coef, values, half):
    re, im = values[:half], values[half:]
    cr, ci = coef
    return jnp.concatenate([cr * re - ci * im, cr * im + ci * re], 0)


def sweep_kernel(
    segs, parts, axial_ref, angle_ref, area_ref, inc_ref, lit_ref, end_ref, out_ref,
    geo, tfeat, sfeat, q0, soft0, q1, soft1, table0, table1, cur1, cur2, state,
    geo_send, geo_recv, send_sem, recv_sem,
):
    seg, part = lax.axis_index("seg"), lax.axis_index("patch")
    patches = axial_ref.shape[1]
    tiles = patches // TILE
    half = inc_ref.shape[1] // 4
    after, before = lax.rem(seg + 1, segs), lax.rem(seg + segs - 1, segs)

    barrier = pltpu.get_barrier_semaphore()

    def greet(k, _):
        for other in (before, after):
            pl.semaphore_signal(barrier, inc=1, device_id=(other, k), device_id_type=MESH)
        return 0

    lax.fori_loop(0, parts, greet, 0)
    pl.semaphore_wait(barrier, 2 * parts)

    geo_copies = []
    for c, ref in enumerate((axial_ref, angle_ref, area_ref)):
        for d, other in ((0, after), (1, before)):
            copy = pltpu.make_async_remote_copy(
                src_ref=ref, dst_ref=geo.at[d, c],
                send_sem=geo_send.at[d, c], recv_sem=geo_recv.at[d, c],
                device_id=(other, part), device_id_type=MESH,
            )
            copy.start()
            geo_copies.append(copy)

    def send_currents(source, sweep, blocks):
        def one(k, _):
            other_part = lax.rem(part + k, parts)
            for d, other in ((0, after), (1, before)):
                pltpu.make_async_remote_copy(
                    src_ref=source.at[pl.ds(2 * half * d, 2 * half), :],
                    dst_ref=blocks.at[d, part],
                    send_sem=send_sem.at[sweep, d], recv_sem=recv_sem.at[sweep, d],
                    device_id=(other, other_part), device_id_type=MESH,
                ).start()
            return 0

        lax.fori_loop(0, parts, one, 0)

    def all_blocks(sweep, d, blocks):
        return pltpu.make_async_remote_copy(
            src_ref=blocks.at[d], dst_ref=blocks.at[d],
            send_sem=send_sem.at[sweep, d], recv_sem=recv_sem.at[sweep, d],
            device_id=(after, part), device_id_type=MESH,
        )

    send_currents(inc_ref.at[0], 0, cur1)

    at = pl.ds(pl.multiple_of(part * TILE, TILE), TILE)
    own_axial = jnp.broadcast_to(axial_ref[:, at], (8, TILE))
    own_angle = jnp.broadcast_to(angle_ref[:, at], (8, TILE))
    for d in (0, 1):
        target_features(own_axial, own_angle, tfeat, d)
    for copy in geo_copies:
        copy.wait_recv()

    tables = (table0, table1)
    for d in (0, 1):
        source_features(geo, lit_ref, sfeat, d, patches)
        build_tables(d, tfeat, sfeat, ((q0, soft0), (q1, soft1)), tables, tiles)

    first = (column(end_ref[0:1, :], 0, half), column(end_ref[0:1, :], half, half))
    last = (column(end_ref[1:2, :], 0, half), column(end_ref[1:2, :], half, half))
    incident = inc_ref[0].astype(f32)
    at_first, at_last = seg == 0, seg == segs - 1
    current = incident
    for sweep, blocks in ((0, cur1), (1, cur2)):
        for d in (0, 1):
            all_blocks(sweep, d, blocks).wait_recv()
        forward = couple(0, blocks, tables, tiles, half)
        backward = couple(1, blocks, tables, tiles, half)
        forward = jnp.where(at_first, reflect(first, current[2 * half :], half), forward)
        backward = jnp.where(at_last, reflect(last, current[: 2 * half], half), backward)
        total = (incident + jnp.concatenate([forward, backward], 0)).astype(bf16)
        if sweep == 0:
            state[...] = total
            current = total.astype(f32)
            send_currents(state, 1, cur2)
        else:
            out_ref[0] = total
    for copy in geo_copies:
        copy.wait_send()
    for sweep, blocks in ((0, cur1), (1, cur2)):
        for d in (0, 1):
            all_blocks(sweep, d, blocks).wait_send()


def on_device(segs, parts, incident, wall_axial, wall_angle, wall_area, visibility, end_reflection):
    channels, width = incident.shape[1:]
    patches = wall_axial.shape[1]
    half = channels // 4
    tiles = patches // TILE
    vmem = pl.BlockSpec(memory_space=pltpu.VMEM)
    buffer = pltpu.VMEM((TILE, TILE), f32)
    table = pltpu.VMEM((tiles, TILE, 2 * TILE), bf16)
    blocks = pltpu.VMEM((2, parts, 2 * half, width), bf16)
    return pl.pallas_call(
        functools.partial(sweep_kernel, segs, parts),
        out_shape=jax.ShapeDtypeStruct(incident.shape, bf16),
        in_specs=[vmem] * 4 + [pl.BlockSpec(memory_space=pltpu.SMEM), vmem],
        out_specs=vmem,
        scratch_shapes=[
            pltpu.VMEM((2, 3, 1, patches), f32),
            pltpu.VMEM((2, TILE, 8 * GROUPS), bf16),
            pltpu.VMEM((2, 2, 8 * GROUPS, patches), bf16),
            buffer, buffer, buffer, buffer, table, table, blocks, blocks,
            pltpu.VMEM((channels, width), bf16),
            pltpu.SemaphoreType.DMA((2, 3)),
            pltpu.SemaphoreType.DMA((2, 3)),
            pltpu.SemaphoreType.DMA((2, 2)),
            pltpu.SemaphoreType.DMA((2, 2)),
        ],
        compiler_params=pltpu.CompilerParams(
            collective_id=0, has_side_effects=True, vmem_limit_bytes=48 << 20
        ),
    )(wall_axial, wall_angle, wall_area, incident, visibility, end_reflection)


def solution(mesh):
    return jax.shard_map(
        functools.partial(on_device, mesh.shape["seg"], mesh.shape["patch"]),
        mesh=mesh,
        in_specs=(
            P("seg", None, "patch"),
            P("seg", None),
            P("seg", None),
            P("seg", None),
            P("seg", None, "patch", None),
            P(),
        ),
        out_specs=P("seg", None, "patch"),
        check_vma=False,
    )
```

time: 165 us -> 57.8 us (0.35)
  the two profiles are of different devices: /device:TPU:207 before, /device:TPU:16 now
where the time goes in v1:
time: 57.8 us; the launch traced here: 57.4 us
  Pallas kernels  52.5 us (91%)
  local copies, waits for them, and re-layouts  4.88 us (8%)
    pallas_call x1, Pallas kernels, on_device(): pl.pallas_call(functools.partial(sweep_kernel, segs, parts), out_shape=ja...  52.5 us
    unnamed x13, local copies, waits for them, and re-layouts  4.88 us

profile of v1, /device:TPU:16, one launch (start us, length us, event | category | flops | bytes accessed | tf_op | source)
XLA Modules:
  0.0 57.4 jit_solution(11257474922064122756)
XLA Ops:
  0.0 0.0 copy-start
  0.0 0.8 %copy-done = bf16[1,64,256]{2,1,0:T(8,128)(2,1)S(1)} copy-done((bf16[1,64,256]{2,1,0:T(8,128)(2,1)S(1)}, bf16[1,64,256]{2,1,0:T(8,128)(2,1)}, u32[]{:S(2)}) %copy-start) | copy-done | bytes 32792
  0.8 0.0 copy-start.1
  0.8 0.7 %copy-done.1 = f32[1,4096]{1,0:T(1,128)S(1)} copy-done((f32[1,4096]{1,0:T(1,128)S(1)}, f32[1,4096]{1,0:T(1,128)}, u32[]{:S(2)}) %copy-start.1) | copy-done | bytes 16408
  1.5 0.0 copy-start.2
  1.5 0.7 %copy-done.2 = f32[1,4096]{1,0:T(1,128)S(1)} copy-done((f32[1,4096]{1,0:T(1,128)S(1)}, f32[1,4096]{1,0:T(1,128)}, u32[]{:S(2)}) %copy-start.2) | copy-done | bytes 16408
  2.2 0.0 copy-start.3
  2.2 0.7 %copy-done.3 = f32[1,4096]{1,0:T(1,128)S(1)} copy-done((f32[1,4096]{1,0:T(1,128)S(1)}, f32[1,4096]{1,0:T(1,128)}, u32[]{:S(2)}) %copy-start.3) | copy-done | bytes 16408
  2.9 0.0 copy-start.4
  2.9 0.7 %copy-done.4 = s32[1,2,2,32]{3,2,1,0:T(2,128)S(1)} copy-done((s32[1,2,2,32]{3,2,1,0:T(2,128)S(1)}, s32[1,2,2,32]{3,2,1,0:T(2,128)}, u32[]{:S(2)}) %copy-start.4) | copy-done | bytes 536
  3.6 0.0 copy-start.5
  3.6 0.7 %copy-done.5 = f32[2,32]{1,0:T(2,128)S(1)} copy-done((f32[2,32]{1,0:T(2,128)S(1)}, f32[2,32]{1,0:T(2,128)}, u32[]{:S(2)}) %copy-start.5) | copy-done | bytes 280
  4.3 52.5 %shard_map.64 = bf16[1,64,256]{2,1,0:T(8,128)(2,1)S(1)} custom-call(f32[1,4096]{1,0:T(1,128)S(1)} %copy-done.1, f32[1,4096]{1,0:T(1,128)S(1)} %copy-done.2, f32[1,4096]{1,0:T(1,128)S(1)} %copy-done.3, bf16[1,64,256]{2,1,0:T(8,128)(2,1)S(1)} %copy-done, s32[1,2,2,32]{3,2,1,0:T(2,128)S(1)} %copy-done.4, f32[2,32]{1,0:T(2,128)S(1)} %copy-done.5), custom_call_target="tpu_custom_call" | custom-call | tf_op jit(solution)/shard_map/pallas_call | solution.py:268
  56.7 0.6 %copy.8 = bf16[1,64,256]{2,1,0:T(8,128)(2,1)} copy(bf16[1,64,256]{2,1,0:T(8,128)(2,1)S(1)} %shard_map.64) | data formatting | bytes 65536
Async XLA Ops:
  0.0 0.8 %copy-start = (bf16[1,64,256]{2,1,0:T(8,128)(2,1)S(1)}, bf16[1,64,256]{2,1,0:T(8,128)(2,1)}, u32[]{:S(2)}) copy-start(bf16[1,64,256]{2,1,0:T(8,128)(2,1)} %inc_ref.1) | copy-start | bytes 98308
  0.8 0.7 %copy-start.1 = (f32[1,4096]{1,0:T(1,128)S(1)}, f32[1,4096]{1,0:T(1,128)}, u32[]{:S(2)}) copy-start(f32[1,4096]{1,0:T(1,128)} %axial_ref.1) | copy-start | bytes 49156
  1.5 0.7 %copy-start.2 = (f32[1,4096]{1,0:T(1,128)S(1)}, f32[1,4096]{1,0:T(1,128)}, u32[]{:S(2)}) copy-start(f32[1,4096]{1,0:T(1,128)} %angle_ref.1) | copy-start | bytes 49156
  2.2 0.7 %copy-start.3 = (f32[1,4096]{1,0:T(1,128)S(1)}, f32[1,4096]{1,0:T(1,128)}, u32[]{:S(2)}) copy-start(f32[1,4096]{1,0:T(1,128)} %area_ref.1) | copy-start | bytes 49156
  2.9 0.7 %copy-start.4 = (s32[1,2,2,32]{3,2,1,0:T(2,128)S(1)}, s32[1,2,2,32]{3,2,1,0:T(2,128)}, u32[]{:S(2)}) copy-start(s32[1,2,2,32]{3,2,1,0:T(2,128)} %lit_ref.1) | copy-start | bytes 1540
  3.6 0.7 %copy-start.5 = (f32[2,32]{1,0:T(2,128)S(1)}, f32[2,32]{1,0:T(2,128)}, u32[]{:S(2)}) copy-start(f32[2,32]{1,0:T(2,128)} %end_ref.1) | copy-start | bytes 772

commit v2 on v1

v2 whole, which is shorter than its diff:
```python
import functools
import math

import jax
import jax.numpy as jnp
from jax import lax
from jax.experimental import pallas as pl
from jax.experimental.pallas import tpu as pltpu
from jax.sharding import PartitionSpec as P

ITERS = 2
WAVENUMBER = 40.0
RADIUS = 0.5
SOFTENING = 0.25

MESH = pl.DeviceIdType.MESH
f32, bf16 = jnp.float32, jnp.bfloat16
NT = (((1,), (1,)), ((), ()))

KAPPA = WAVENUMBER / (2.0 * math.pi)
KAPPA2 = KAPPA * KAPPA
CHORD = 2.0 * RADIUS * RADIUS * KAPPA2
ROOT_CHORD = math.sqrt(CHORD)
MAGIC = 12582912.0
DARK = 2.0**127
SIN = (4.441535736857015, -7.264681196614785, 3.252051034939137)
COS = (1.4142040822010087, -6.977642112452626, 5.715238841259401, -1.728349684464805)
TURN = (
    6.283185306487509,
    -41.341701929774175,
    81.60520943123053,
    -76.70366783378654,
    41.999989934944594,
    -14.337025371611837,
)
TILE = 256
ROWS = 32
GROUPS = 6


def poly(x, coefs):
    total = coefs[-1]
    for c in coefs[-2::-1]:
        total = c + x * total
    return total


def split3(x):
    hi = x.astype(bf16).astype(f32)
    rest = x - hi
    mid = rest.astype(bf16).astype(f32)
    return hi, mid, rest - mid


def trig_rows(angle, row):
    g = angle * (0.5 / math.pi) + jnp.where(row == 3, 0.25, 0.0)
    g = jnp.where(g > 0.5, g - 1.0, g)
    h = jnp.where(g > 0.25, 0.5 - g, jnp.where(g < -0.25, -0.5 - g, g))
    return h * poly(h * h, TURN)


def target_features(axial, angle, into, slot, away):
    width = axial.shape[1]
    row = lax.broadcasted_iota(jnp.int32, (8, width), 0)
    lane = lax.broadcasted_iota(jnp.int32, (8, width), 1)
    a = KAPPA * (axial if not away else 1.0 - axial)
    q = jnp.where(row == 0, a * a, jnp.where(row == 1, a, 1.0))
    q = jnp.where(row >= 3, ROOT_CHORD * trig_rows(angle, row), q)
    block = jnp.where(lane < width // 2, 5, 6)
    q = jnp.where(row >= 5, jnp.where(row == block, 2.0, 0.0), q)
    hi, mid, low = split3(q)
    full = jnp.concatenate([hi, hi, hi, mid, mid, low], 0)
    full = jnp.concatenate([full, jnp.zeros((128 - 8 * GROUPS, width), f32)], 0)
    into[slot] = full.T[:, : 8 * GROUPS].astype(bf16)


def source_features(geo, slot, d, lit, into, patches):
    row = lax.broadcasted_iota(jnp.int32, (8, 128), 0)
    turned = (1 - d).astype(f32)
    sign = 1.0 - 2.0 * turned

    def block(jb, _):
        sl = pl.ds(pl.multiple_of(jb * 128, 128), 128)
        axial = jnp.broadcast_to(geo[slot, 0, :, sl], (8, 128))
        angle = jnp.broadcast_to(geo[slot, 1, :, sl], (8, 128))
        area = jnp.broadcast_to(geo[slot, 2, :, sl], (8, 128))
        b = KAPPA * (turned + sign * axial)
        bb = b * b + CHORD
        low_rows = jnp.where(row == 0, 1.0, jnp.where(row == 1, 2.0 * b, bb))
        trig = jnp.where(row >= 5, 0.0, -ROOT_CHORD * trig_rows(angle, row))
        q = jnp.where(row >= 3, trig, low_rows)
        weight = (patches / KAPPA2) / (area * area)
        soft = jnp.where(row == 2, q + SOFTENING * KAPPA2, q) * weight
        dark0 = (1 - lit[0, d, 0, jb]).astype(f32) * DARK
        dark1 = (1 - lit[0, d, 1, jb]).astype(f32) * DARK
        soft = jnp.where(row == 5, dark0, jnp.where(row == 6, dark1, soft))
        for which, value in ((0, q), (1, soft)):
            hi, mid, low = split3(value)
            into[slot, which, :, sl] = jnp.concatenate([hi, mid, low, hi, mid, hi], 0).astype(bf16)
        return 0

    lax.fori_loop(0, patches // 128, block, 0, unroll=4)


def kernel_tile(q_ref, soft_ref, table, at):
    for i0 in range(0, TILE, ROWS):
        sl = pl.ds(i0, ROWS)
        q = jnp.maximum(q_ref[sl, :], 1e-30)
        m = lax.rsqrt(soft_ref[sl, :])
        t = q * lax.rsqrt(q)
        f = t - ((t + MAGIC) - MAGIC)
        ff = f * f
        s = f * poly(ff, SIN)
        c = poly(ff, COS)
        u = m * s
        table[at, sl, 0:TILE] = (m - u * s).astype(bf16)
        table[at, sl, TILE : 2 * TILE] = (u * c).astype(bf16)


def distances(feat, sfeat, slot, tile, pair):
    js = pl.ds(pl.multiple_of(tile * TILE, TILE), TILE)
    for which in (0, 1):
        pair[which][...] = jnp.dot(feat, sfeat[slot, which, :, js], preferred_element_type=f32)


def build_tables(feat, sfeat, slot, buffers, tables, tiles, first, last):
    def step(k, _):
        distances(feat[...], sfeat, slot, 2 * k + 1, buffers[1])
        kernel_tile(*buffers[0], tables[0], slot * (tiles // 2) + k)
        distances(feat[...], sfeat, slot, jnp.minimum(2 * k + 2, tiles - 1), buffers[0])
        kernel_tile(*buffers[1], tables[1], slot * (tiles // 2) + k)
        return 0

    lax.fori_loop(first, last, step, 0)


def couple(blocks, slot, tables, tiles, half):
    def product(k, par):
        c = blocks[slot, 2 * k + par]
        turned = jnp.concatenate([c[half:], -c[:half]], 0)
        both = jnp.concatenate([c, turned], 1)
        table = tables[par][slot * (tiles // 2) + k]
        return lax.dot_general(both, table, NT, preferred_element_type=f32)

    def step(k, total):
        return total + product(k, 0) + product(k, 1)

    return lax.fori_loop(0, tiles // 2, step, jnp.zeros((2 * half, TILE), f32), unroll=8)


def column(row_values, start, count):
    row = lax.broadcasted_iota(jnp.int32, (count, row_values.shape[1]), 0)
    lane = lax.broadcasted_iota(jnp.int32, (count, row_values.shape[1]), 1)
    wide = jnp.broadcast_to(row_values, (count, row_values.shape[1]))
    return jnp.sum(jnp.where(lane == row + start, wide, 0.0), axis=1, keepdims=True)


def reflect(coef, values, half):
    re, im = values[:half], values[half:]
    cr, ci = coef
    return jnp.concatenate([cr * re - ci * im, cr * im + ci * re], 0)


NEAR, FAR = 0, 1


def sweep_kernel(
    segs, parts, axial_hbm, angle_hbm, area_hbm, inc_hbm, lit_hbm, end_hbm, out_ref,
    own, inc, end, lit, geo, tfeat, sfeat, q0, soft0, q1, soft1, table0, table1, cur1, cur2, state,
    in_sem, geo_send, geo_recv, shift_send, shift_recv, plane_send, plane_recv,
):
    seg, part = lax.axis_index("seg"), lax.axis_index("patch")
    patches = axial_hbm.shape[1]
    tiles = patches // TILE
    half = inc_hbm.shape[1] // 4
    core = lax.rem(seg, 2)
    near = seg + 1 - 2 * core
    far = seg - 1 + 2 * core
    has_far = jnp.logical_and(far >= 0, far < segs)
    d_near, d_far = 1 - core, core

    loads = [
        pltpu.make_async_copy(src, dst, in_sem.at[n])
        for n, (src, dst) in enumerate((
            (axial_hbm, own.at[0]), (angle_hbm, own.at[1]), (area_hbm, own.at[2]),
            (inc_hbm.at[0], inc), (end_hbm, end), (lit_hbm, lit),
        ))
    ]
    for load in loads:
        load.start()

    barrier = pltpu.get_barrier_semaphore()

    def greet(k, _):
        other = lax.rem(part + k, parts)
        pl.semaphore_signal(barrier, inc=1, device_id=(seg, other), device_id_type=MESH)
        return 0

    pl.semaphore_signal(barrier, inc=1, device_id=(near, part), device_id_type=MESH)

    @pl.when(has_far)
    def _():
        pl.semaphore_signal(barrier, inc=1, device_id=(far, part), device_id_type=MESH)

    lax.fori_loop(1, parts, greet, 0)

    for load in loads:
        load.wait()
    at = pl.ds(pl.multiple_of(part * TILE, TILE), TILE)
    own_axial = jnp.broadcast_to(own[0, :, at], (8, TILE))
    own_angle = jnp.broadcast_to(own[1, :, at], (8, TILE))
    for d in (0, 1):
        target_features(own_axial, own_angle, tfeat, d, d == 1)

    @pl.when(jnp.logical_not(has_far))
    def _():
        geo[FAR] = jnp.ones_like(geo[FAR])
        cur1[FAR] = jnp.zeros_like(cur1[FAR])
        cur2[FAR] = jnp.zeros_like(cur2[FAR])

    pl.semaphore_wait(barrier, parts + has_far.astype(jnp.int32))

    def geometry(slot):
        return [
            pltpu.make_async_remote_copy(
                src_ref=own.at[c], dst_ref=geo.at[slot, c],
                send_sem=geo_send.at[slot, c], recv_sem=geo_recv.at[slot, c],
                device_id=(near if slot == NEAR else far, part), device_id_type=MESH,
            )
            for c in range(3)
        ]

    def shift(source, sweep, blocks, slot):
        d = d_far if slot == NEAR else d_near
        return pltpu.make_async_remote_copy(
            src_ref=source.at[pl.ds(pl.multiple_of(2 * half * d, 2 * half), 2 * half), :],
            dst_ref=blocks.at[slot, part],
            send_sem=shift_send.at[sweep, slot], recv_sem=shift_recv.at[sweep, slot],
            device_id=(near if slot == NEAR else far, part), device_id_type=MESH,
        )

    def pass_on(sweep, blocks, slot):
        def one(k, _):
            other = lax.rem(part + k, parts)
            pltpu.make_async_remote_copy(
                src_ref=blocks.at[slot, part], dst_ref=blocks.at[slot, part],
                send_sem=plane_send.at[sweep, slot], recv_sem=plane_recv.at[sweep, slot],
                device_id=(seg, other), device_id_type=MESH,
            ).start()
            return 0

        lax.fori_loop(1, parts, one, 0)

    def plane(sweep, blocks, slot):
        most = blocks.at[slot, pl.ds(0, parts - 1)]
        return pltpu.make_async_remote_copy(
            src_ref=most, dst_ref=most,
            send_sem=plane_send.at[sweep, slot], recv_sem=plane_recv.at[sweep, slot],
            device_id=(near, part), device_id_type=MESH,
        )

    def if_far(act):
        pl.when(has_far)(act)

    near_geo, far_geo = geometry(NEAR), geometry(FAR)
    for copy in near_geo:
        copy.start()
    shift(inc, 0, cur1, NEAR).start()

    @if_far
    def _():
        shift(inc, 0, cur1, FAR).start()
        for copy in far_geo:
            copy.start()

    tables = (table0, table1)
    buffers = ((q0, soft0), (q1, soft1))
    near_feat, far_feat = tfeat.at[d_near], tfeat.at[d_far]

    shift(inc, 0, cur1, NEAR).wait_recv()
    pass_on(0, cur1, NEAR)
    for copy in near_geo:
        copy.wait_recv()
    source_features(geo, NEAR, d_near, lit, sfeat, patches)
    distances(near_feat[...], sfeat, NEAR, 0, buffers[0])
    build_tables(near_feat, sfeat, NEAR, buffers, tables, tiles, 0, tiles // 4)

    @if_far
    def _():
        shift(inc, 0, cur1, FAR).wait_recv()
        pass_on(0, cur1, FAR)

    build_tables(near_feat, sfeat, NEAR, buffers, tables, tiles, tiles // 4, tiles // 2)

    first = (column(end[0:1, :], 0, half), column(end[0:1, :], half, half))
    last = (column(end[1:2, :], 0, half), column(end[1:2, :], half, half))
    is_first = (core == 0).astype(f32)
    mirror = [is_first * f + (1.0 - is_first) * l for f, l in zip(first, last)]

    def rows(d):
        return pl.ds(pl.multiple_of(2 * half * d, 2 * half), 2 * half)

    def near_sum(blocks):
        return inc[rows(d_near), :].astype(f32) + couple(blocks, NEAR, tables, tiles, half)

    def far_sum(blocks, previous):
        coupled = couple(blocks, FAR, tables, tiles, half)
        mirrored = reflect(mirror, previous[rows(d_near), :].astype(f32), half)
        return inc[rows(d_far), :].astype(f32) + jnp.where(has_far, coupled, mirrored)

    plane(0, cur1, NEAR).wait_recv()
    state[rows(d_near), :] = near_sum(cur1).astype(bf16)

    @if_far
    def _():
        shift(state, 1, cur2, FAR).start()
        for copy in far_geo:
            copy.wait_recv()

    source_features(geo, FAR, d_far, lit, sfeat, patches)
    distances(far_feat[...], sfeat, FAR, 0, buffers[0])
    build_tables(far_feat, sfeat, FAR, buffers, tables, tiles, 0, 3 * tiles // 8)

    @if_far
    def _():
        shift(state, 1, cur2, FAR).wait_recv()
        pass_on(1, cur2, FAR)

    build_tables(far_feat, sfeat, FAR, buffers, tables, tiles, 3 * tiles // 8, tiles // 2)

    @if_far
    def _():
        plane(0, cur1, FAR).wait_recv()

    state[rows(d_far), :] = far_sum(cur1, inc).astype(bf16)
    shift(state, 1, cur2, NEAR).start()
    shift(state, 1, cur2, NEAR).wait_recv()
    pass_on(1, cur2, NEAR)

    @if_far
    def _():
        plane(1, cur2, FAR).wait_recv()

    out_ref[0, rows(d_far), :] = far_sum(cur2, state).astype(bf16)
    plane(1, cur2, NEAR).wait_recv()
    out_ref[0, rows(d_near), :] = near_sum(cur2).astype(bf16)

    for copy in near_geo:
        copy.wait_send()
    for sweep, source, blocks in ((0, inc, cur1), (1, state, cur2)):
        shift(source, sweep, blocks, NEAR).wait_send()
        plane(sweep, blocks, NEAR).wait_send()

    @if_far
    def _():
        for copy in far_geo:
            copy.wait_send()
        for sweep, source, blocks in ((0, inc, cur1), (1, state, cur2)):
            shift(source, sweep, blocks, FAR).wait_send()
            plane(sweep, blocks, FAR).wait_send()


def on_device(segs, parts, incident, wall_axial, wall_angle, wall_area, visibility, end_reflection):
    channels, width = incident.shape[1:]
    patches = wall_axial.shape[1]
    half = channels // 4
    tiles = patches // TILE
    buffer = pltpu.VMEM((TILE, TILE), f32)
    table = pltpu.VMEM((tiles, TILE, 2 * TILE), bf16)
    blocks = pltpu.VMEM((2, parts, 2 * half, width), bf16)
    rows = pltpu.VMEM((channels, width), bf16)
    return pl.pallas_call(
        functools.partial(sweep_kernel, segs, parts),
        out_shape=jax.ShapeDtypeStruct(incident.shape, bf16),
        in_specs=[pl.BlockSpec(memory_space=pl.ANY)] * 6,
        out_specs=pl.BlockSpec(memory_space=pltpu.VMEM),
        scratch_shapes=[
            pltpu.VMEM((3, 1, patches), f32),
            rows,
            pltpu.VMEM(end_reflection.shape, f32),
            pltpu.SMEM(visibility.shape, jnp.int32),
            pltpu.VMEM((2, 3, 1, patches), f32),
            pltpu.VMEM((2, TILE, 8 * GROUPS), bf16),
            pltpu.VMEM((2, 2, 8 * GROUPS, patches), bf16),
            buffer, buffer, buffer, buffer, table, table, blocks, blocks, rows,
            pltpu.SemaphoreType.DMA((6,)),
            pltpu.SemaphoreType.DMA((2, 3)),
            pltpu.SemaphoreType.DMA((2, 3)),
            pltpu.SemaphoreType.DMA((2, 2)),
            pltpu.SemaphoreType.DMA((2, 2)),
            pltpu.SemaphoreType.DMA((2, 2)),
            pltpu.SemaphoreType.DMA((2, 2)),
        ],
        compiler_params=pltpu.CompilerParams(
            collective_id=0, has_side_effects=True, vmem_limit_bytes=56 << 20
        ),
    )(wall_axial, wall_angle, wall_area, incident, visibility, end_reflection)


def solution(mesh):
    return jax.shard_map(
        functools.partial(on_device, mesh.shape["seg"], mesh.shape["patch"]),
        mesh=mesh,
        in_specs=(
            P("seg", None, "patch"),
            P("seg", None),
            P("seg", None),
            P("seg", None),
            P("seg", None, "patch", None),
            P(),
        ),
        out_specs=P("seg", None, "patch"),
        check_vma=False,
    )
```

time: 57.8 us -> 43 us (0.74)
  the two profiles are of different devices: /device:TPU:16 before, /device:TPU:321 now
where the time goes in v2:
time: 43 us; the launch traced here: 42.8 us
  Pallas kernels  41.4 us (96%)
  local copies, waits for them, and re-layouts  1.38 us (3%)
    pallas_call x1, Pallas kernels, on_device(): pl.pallas_call(functools.partial(sweep_kernel, segs, parts), out_shape=ja...  41.4 us
    unnamed x1, local copies, waits for them, and re-layouts  1.38 us

profile of v2, /device:TPU:321, one launch (start us, length us, event | category | flops | bytes accessed | tf_op | source)
XLA Modules:
  0.0 42.8 jit_solution(15327548325559446276)
XLA Ops:
  0.0 41.4 %shard_map.64 = bf16[1,64,256]{2,1,0:T(8,128)(2,1)} custom-call(f32[1,4096]{1,0:T(1,128)} %axial_hbm.1, f32[1,4096]{1,0:T(1,128)} %angle_hbm.1, f32[1,4096]{1,0:T(1,128)} %area_hbm.1, bf16[1,64,256]{2,1,0:T(8,128)(2,1)} %inc_hbm.1, s32[1,2,2,32]{3,2,1,0:T(2,128)} %lit_hbm.1, f32[2,32]{1,0:T(2,128)} %end_hbm.1), custom_call_target="tpu_custom_call" | custom-call | tf_op jit(solution)/shard_map/pallas_call | solution.py:372
  41.4 1.4 %copy.8 = bf16[1,64,256]{2,1,0:T(8,128)(2,1)} copy(bf16[1,64,256]{2,1,0:T(8,128)(2,1)} %shard_map.64) | data formatting | bytes 65536

commit v3 on v2

--- a/solution.py
+++ b/solution.py
@@ -123,29 +123,32 @@
         pair[which][...] = jnp.dot(feat, sfeat[slot, which, :, js], preferred_element_type=f32)
 
 
-def build_tables(feat, sfeat, slot, buffers, tables, tiles, first, last):
+def build_table(feat, sfeat, slot, buffers, table, tiles, first, last, beside):
     def step(k, _):
+        beside(k, 0)
         distances(feat[...], sfeat, slot, 2 * k + 1, buffers[1])
-        kernel_tile(*buffers[0], tables[0], slot * (tiles // 2) + k)
+        kernel_tile(*buffers[0], table, 2 * k)
+        beside(k, 1)
         distances(feat[...], sfeat, slot, jnp.minimum(2 * k + 2, tiles - 1), buffers[0])
-        kernel_tile(*buffers[1], tables[1], slot * (tiles // 2) + k)
+        kernel_tile(*buffers[1], table, 2 * k + 1)
         return 0
 
+    if first == 0:
+        distances(feat[...], sfeat, slot, 0, buffers[0])
     lax.fori_loop(first, last, step, 0)
 
 
-def couple(blocks, slot, tables, tiles, half):
-    def product(k, par):
-        c = blocks[slot, 2 * k + par]
-        turned = jnp.concatenate([c[half:], -c[:half]], 0)
-        both = jnp.concatenate([c, turned], 1)
-        table = tables[par][slot * (tiles // 2) + k]
-        return lax.dot_general(both, table, NT, preferred_element_type=f32)
-
+def product(block, table, half):
+    turned = jnp.concatenate([block[half:], -block[:half]], 0)
+    both = jnp.concatenate([block, turned], 1)
+    return lax.dot_general(both, table, NT, preferred_element_type=f32)
+
+
+def couple(blocks, slot, table, base, count, half):
     def step(k, total):
-        return total + product(k, 0) + product(k, 1)
-
-    return lax.fori_loop(0, tiles // 2, step, jnp.zeros((2 * half, TILE), f32), unroll=8)
+        return total + product(blocks[slot, base + k], table[base + k], half)
+
+    return lax.fori_loop(0, count, step, jnp.zeros((2 * half, TILE), f32), unroll=4)
 
 
 def column(row_values, start, count):
@@ -166,8 +169,8 @@
 
 def sweep_kernel(
     segs, parts, axial_hbm, angle_hbm, area_hbm, inc_hbm, lit_hbm, end_hbm, out_ref,
-    own, inc, end, lit, geo, tfeat, sfeat, q0, soft0, q1, soft1, table0, table1, cur1, cur2, state,
-    in_sem, geo_send, geo_recv, shift_send, shift_recv, plane_send, plane_recv,
+    own, inc, end, lit, geo, tfeat, sfeat, q0, soft0, q1, soft1, near_table, far_table, cur1, cur2, state, total,
+    in_sem, geo_send, geo_recv, sent, row_recv, side_recv,
 ):
     seg, part = lax.axis_index("seg"), lax.axis_index("patch")
     patches = axial_hbm.shape[1]
@@ -191,18 +194,91 @@
 
     barrier = pltpu.get_barrier_semaphore()
 
-    def greet(k, _):
-        other = lax.rem(part + k, parts)
-        pl.semaphore_signal(barrier, inc=1, device_id=(seg, other), device_id_type=MESH)
-        return 0
-
-    pl.semaphore_signal(barrier, inc=1, device_id=(near, part), device_id_type=MESH)
+    ring = parts // 2
+    place, side = lax.rem(part, ring), part // ring
+    own_base, other_base = side * ring, (1 - side) * ring
+    across = other_base + place
+
+    def in_row(base, n):
+        return base + lax.rem(place + n, ring)
+
+    for n in range(ring):
+        pl.semaphore_signal(barrier, inc=1, device_id=(near, in_row(own_base, n)), device_id_type=MESH)
+    pl.semaphore_signal(barrier, inc=1, device_id=(seg, across), device_id_type=MESH)
 
     @pl.when(has_far)
     def _():
-        pl.semaphore_signal(barrier, inc=1, device_id=(far, part), device_id_type=MESH)
-
-    lax.fori_loop(1, parts, greet, 0)
+        for n in range(ring):
+            pl.semaphore_signal(barrier, inc=1, device_id=(far, in_row(other_base, n)), device_id_type=MESH)
+
+    @pl.when(jnp.logical_not(has_far))
+    def _():
+        geo[FAR] = jnp.ones_like(geo[FAR])
+        cur1[FAR] = jnp.zeros_like(cur1[FAR])
+        cur2[FAR] = jnp.zeros_like(cur2[FAR])
+
+    pl.semaphore_wait(barrier, ring + 1 + ring * has_far.astype(jnp.int32))
+
+    def geometry(slot):
+        return [
+            pltpu.make_async_remote_copy(
+                src_ref=ref, dst_ref=geo.at[slot, c],
+                send_sem=geo_send.at[slot, c], recv_sem=geo_recv.at[slot, c],
+                device_id=(near, part) if slot == NEAR else (far, across), device_id_type=MESH,
+            )
+            for c, ref in enumerate((axial_hbm, angle_hbm, area_hbm))
+        ]
+
+    steps = [n for k in range(1, ring // 2) for n in (k, ring - k)] + [ring // 2]
+
+    def spread(source, sweep, blocks, slot):
+        d = d_far if slot == NEAR else d_near
+        for n in [*steps[::-1], 0]:
+            pltpu.make_async_remote_copy(
+                src_ref=source.at[pl.ds(pl.multiple_of(2 * half * d, 2 * half), 2 * half), :],
+                dst_ref=blocks.at[slot, part],
+                send_sem=sent.at[sweep, slot], recv_sem=row_recv.at[sweep, slot, n],
+                device_id=(near, in_row(own_base, n)) if slot == NEAR else (far, in_row(other_base, n)),
+                device_id_type=MESH,
+            ).start()
+
+    def hand_across(sweep, blocks, slot, which):
+        for n in which:
+            block = blocks.at[slot, in_row(own_base if slot == NEAR else other_base, ring - n)]
+
+            def copy(recv):
+                return pltpu.make_async_remote_copy(
+                    src_ref=block, dst_ref=block, send_sem=sent.at[sweep, slot], recv_sem=recv,
+                    device_id=(seg, across), device_id_type=MESH,
+                )
+
+            copy(row_recv.at[sweep, slot, n]).wait_recv()
+            copy(side_recv.at[sweep, slot]).start()
+
+    def whole(sweep, blocks, slot, count):
+        some = blocks.at[slot, pl.ds(0, count)]
+        return pltpu.make_async_remote_copy(
+            src_ref=some, dst_ref=some,
+            send_sem=sent.at[sweep, slot], recv_sem=side_recv.at[sweep, slot],
+            device_id=(seg, across), device_id_type=MESH,
+        )
+
+    def handed_here(sweep, blocks, slot):
+        whole(sweep, blocks, slot, ring).wait_recv()
+
+    def if_far(act):
+        pl.when(has_far)(act)
+
+    near_geo, far_geo = geometry(NEAR), geometry(FAR)
+    for copy in near_geo:
+        copy.start()
+    spread(inc_hbm.at[0], 0, cur1, NEAR)
+
+    @if_far
+    def _():
+        for copy in far_geo:
+            copy.start()
+        spread(inc_hbm.at[0], 0, cur1, FAR)
 
     for load in loads:
         load.wait()
@@ -212,152 +288,118 @@
     for d in (0, 1):
         target_features(own_axial, own_angle, tfeat, d, d == 1)
 
-    @pl.when(jnp.logical_not(has_far))
-    def _():
-        geo[FAR] = jnp.ones_like(geo[FAR])
-        cur1[FAR] = jnp.zeros_like(cur1[FAR])
-        cur2[FAR] = jnp.zeros_like(cur2[FAR])
-
-    pl.semaphore_wait(barrier, parts + has_far.astype(jnp.int32))
-
-    def geometry(slot):
-        return [
-            pltpu.make_async_remote_copy(
-                src_ref=own.at[c], dst_ref=geo.at[slot, c],
-                send_sem=geo_send.at[slot, c], recv_sem=geo_recv.at[slot, c],
-                device_id=(near if slot == NEAR else far, part), device_id_type=MESH,
-            )
-            for c in range(3)
-        ]
-
-    def shift(source, sweep, blocks, slot):
-        d = d_far if slot == NEAR else d_near
-        return pltpu.make_async_remote_copy(
-            src_ref=source.at[pl.ds(pl.multiple_of(2 * half * d, 2 * half), 2 * half), :],
-            dst_ref=blocks.at[slot, part],
-            send_sem=shift_send.at[sweep, slot], recv_sem=shift_recv.at[sweep, slot],
-            device_id=(near if slot == NEAR else far, part), device_id_type=MESH,
-        )
-
-    def pass_on(sweep, blocks, slot):
-        def one(k, _):
-            other = lax.rem(part + k, parts)
-            pltpu.make_async_remote_copy(
-                src_ref=blocks.at[slot, part], dst_ref=blocks.at[slot, part],
-                send_sem=plane_send.at[sweep, slot], recv_sem=plane_recv.at[sweep, slot],
-                device_id=(seg, other), device_id_type=MESH,
-            ).start()
-            return 0
-
-        lax.fori_loop(1, parts, one, 0)
-
-    def plane(sweep, blocks, slot):
-        most = blocks.at[slot, pl.ds(0, parts - 1)]
-        return pltpu.make_async_remote_copy(
-            src_ref=most, dst_ref=most,
-            send_sem=plane_send.at[sweep, slot], recv_sem=plane_recv.at[sweep, slot],
-            device_id=(near, part), device_id_type=MESH,
-        )
-
-    def if_far(act):
-        pl.when(has_far)(act)
-
-    near_geo, far_geo = geometry(NEAR), geometry(FAR)
-    for copy in near_geo:
-        copy.start()
-    shift(inc, 0, cur1, NEAR).start()
-
-    @if_far
-    def _():
-        shift(inc, 0, cur1, FAR).start()
-        for copy in far_geo:
-            copy.start()
-
-    tables = (table0, table1)
     buffers = ((q0, soft0), (q1, soft1))
     near_feat, far_feat = tfeat.at[d_near], tfeat.at[d_far]
-
-    shift(inc, 0, cur1, NEAR).wait_recv()
-    pass_on(0, cur1, NEAR)
+    early, late = [0, *steps[:4]], steps[4:]
+    pairs = tiles // 2
+
     for copy in near_geo:
         copy.wait_recv()
     source_features(geo, NEAR, d_near, lit, sfeat, patches)
-    distances(near_feat[...], sfeat, NEAR, 0, buffers[0])
-    build_tables(near_feat, sfeat, NEAR, buffers, tables, tiles, 0, tiles // 4)
-
-    @if_far
-    def _():
-        shift(inc, 0, cur1, FAR).wait_recv()
-        pass_on(0, cur1, FAR)
-
-    build_tables(near_feat, sfeat, NEAR, buffers, tables, tiles, tiles // 4, tiles // 2)
+
+    def beside_near(k, part_of):
+        if part_of:
+            return
+
+        @pl.when(k == pairs // 2)
+        def _():
+            hand_across(0, cur1, NEAR, early)
+
+    build_table(near_feat, sfeat, NEAR, buffers, near_table, tiles, 0, pairs, beside_near)
+    hand_across(0, cur1, NEAR, late)
 
     first = (column(end[0:1, :], 0, half), column(end[0:1, :], half, half))
     last = (column(end[1:2, :], 0, half), column(end[1:2, :], half, half))
     is_first = (core == 0).astype(f32)
     mirror = [is_first * f + (1.0 - is_first) * l for f, l in zip(first, last)]
 
+    @if_far
+    def _():
+        for copy in far_geo:
+            copy.wait_recv()
+
+    source_features(geo, FAR, d_far, lit, sfeat, patches)
+    total[...] = jnp.zeros_like(total)
+
+    def beside_far(k, part_of):
+        if part_of == 0:
+
+            @pl.when(jnp.logical_and(has_far, k == 1))
+            def _():
+                hand_across(0, cur1, FAR, early)
+
+            @pl.when(k == pairs // 4)
+            def _():
+                handed_here(0, cur1, NEAR)
+
+        tile = jnp.where(k < pairs // 4, own_base, other_base - ring) + 4 * k + 2 * part_of
+        for n in (0, 1):
+            total[...] += product(cur1[NEAR, tile + n], near_table[tile + n], half)
+
+    build_table(far_feat, sfeat, FAR, buffers, far_table, tiles, 0, pairs // 2, beside_far)
+
     def rows(d):
         return pl.ds(pl.multiple_of(2 * half * d, 2 * half), 2 * half)
 
-    def near_sum(blocks):
-        return inc[rows(d_near), :].astype(f32) + couple(blocks, NEAR, tables, tiles, half)
-
-    def far_sum(blocks, previous):
-        coupled = couple(blocks, FAR, tables, tiles, half)
+    state[rows(d_near), :] = (inc[rows(d_near), :].astype(f32) + total[...]).astype(bf16)
+
+    @if_far
+    def _():
+        spread(state, 1, cur2, FAR)
+        hand_across(0, cur1, FAR, late)
+
+    build_table(far_feat, sfeat, FAR, buffers, far_table, tiles, pairs // 2, pairs, lambda k, part_of: None)
+
+    def far_result(coupled, previous):
         mirrored = reflect(mirror, previous[rows(d_near), :].astype(f32), half)
-        return inc[rows(d_far), :].astype(f32) + jnp.where(has_far, coupled, mirrored)
-
-    plane(0, cur1, NEAR).wait_recv()
-    state[rows(d_near), :] = near_sum(cur1).astype(bf16)
-
-    @if_far
-    def _():
-        shift(state, 1, cur2, FAR).start()
-        for copy in far_geo:
-            copy.wait_recv()
-
-    source_features(geo, FAR, d_far, lit, sfeat, patches)
-    distances(far_feat[...], sfeat, FAR, 0, buffers[0])
-    build_tables(far_feat, sfeat, FAR, buffers, tables, tiles, 0, 3 * tiles // 8)
-
-    @if_far
-    def _():
-        shift(state, 1, cur2, FAR).wait_recv()
-        pass_on(1, cur2, FAR)
-
-    build_tables(far_feat, sfeat, FAR, buffers, tables, tiles, 3 * tiles // 8, tiles // 2)
-
-    @if_far
-    def _():
-        plane(0, cur1, FAR).wait_recv()
-
-    state[rows(d_far), :] = far_sum(cur1, inc).astype(bf16)
-    shift(state, 1, cur2, NEAR).start()
-    shift(state, 1, cur2, NEAR).wait_recv()
-    pass_on(1, cur2, NEAR)
-
-    @if_far
-    def _():
-        plane(1, cur2, FAR).wait_recv()
-
-    out_ref[0, rows(d_far), :] = far_sum(cur2, state).astype(bf16)
-    plane(1, cur2, NEAR).wait_recv()
-    out_ref[0, rows(d_near), :] = near_sum(cur2).astype(bf16)
+        return (inc[rows(d_far), :].astype(f32) + jnp.where(has_far, coupled, mirrored)).astype(bf16)
+
+    coupled = couple(cur1, FAR, far_table, other_base, ring, half)
+
+    @if_far
+    def _():
+        handed_here(0, cur1, FAR)
+
+    coupled += couple(cur1, FAR, far_table, own_base, ring, half)
+    state[rows(d_far), :] = far_result(coupled, inc)
+    spread(state, 1, cur2, NEAR)
+
+    @if_far
+    def _():
+        hand_across(1, cur2, FAR, early)
+
+    hand_across(1, cur2, NEAR, early)
+
+    @if_far
+    def _():
+        hand_across(1, cur2, FAR, late)
+
+    hand_across(1, cur2, NEAR, late)
+
+    near_coupled = couple(cur2, NEAR, near_table, own_base, ring, half)
+    far_coupled = couple(cur2, FAR, far_table, other_base, ring, half)
+    handed_here(1, cur2, NEAR)
+    near_coupled += couple(cur2, NEAR, near_table, other_base, ring, half)
+    out_ref[0, rows(d_near), :] = (inc[rows(d_near), :].astype(f32) + near_coupled).astype(bf16)
+
+    @if_far
+    def _():
+        handed_here(1, cur2, FAR)
+
+    far_coupled += couple(cur2, FAR, far_table, own_base, ring, half)
+    out_ref[0, rows(d_far), :] = far_result(far_coupled, state)
 
     for copy in near_geo:
         copy.wait_send()
-    for sweep, source, blocks in ((0, inc, cur1), (1, state, cur2)):
-        shift(source, sweep, blocks, NEAR).wait_send()
-        plane(sweep, blocks, NEAR).wait_send()
+    for sweep, blocks in ((0, cur1), (1, cur2)):
+        whole(sweep, blocks, NEAR, parts).wait_send()
 
     @if_far
     def _():
         for copy in far_geo:
             copy.wait_send()
-        for sweep, source, blocks in ((0, inc, cur1), (1, state, cur2)):
-            shift(source, sweep, blocks, FAR).wait_send()
-            plane(sweep, blocks, FAR).wait_send()
+        for sweep, blocks in ((0, cur1), (1, cur2)):
+            whole(sweep, blocks, FAR, parts).wait_send()
 
 
 def on_device(segs, parts, incident, wall_axial, wall_angle, wall_area, visibility, end_reflection):
@@ -383,12 +425,12 @@
             pltpu.VMEM((2, TILE, 8 * GROUPS), bf16),
             pltpu.VMEM((2, 2, 8 * GROUPS, patches), bf16),
             buffer, buffer, buffer, buffer, table, table, blocks, blocks, rows,
+            pltpu.VMEM((2 * half, width), f32),
             pltpu.SemaphoreType.DMA((6,)),
             pltpu.SemaphoreType.DMA((2, 3)),
             pltpu.SemaphoreType.DMA((2, 3)),
             pltpu.SemaphoreType.DMA((2, 2)),
-            pltpu.SemaphoreType.DMA((2, 2)),
-            pltpu.SemaphoreType.DMA((2, 2)),
+            pltpu.SemaphoreType.DMA((2, 2, parts // 2)),
             pltpu.SemaphoreType.DMA((2, 2)),
         ],
         compiler_params=pltpu.CompilerParams(

time: 43 us -> 40.3 us (0.937)
  the two profiles are of different devices: /device:TPU:321 before, /device:TPU:196 now
where the time goes in v3:
time: 40.3 us; the launch traced here: 40.1 us
  Pallas kernels  38.7 us (96%)
  local copies, waits for them, and re-layouts  1.38 us (3%)
    pallas_call x1, Pallas kernels, on_device(): pl.pallas_call(functools.partial(sweep_kernel, segs, parts), out_shape=ja...  38.7 us
    unnamed x1, local copies, waits for them, and re-layouts  1.38 us

profile of v3, /device:TPU:196, one launch (start us, length us, event | category | flops | bytes accessed | tf_op | source)
XLA Modules:
  0.0 40.1 jit_solution(4174790941136114696)
XLA Ops:
  0.0 38.7 %shard_map.64 = bf16[1,64,256]{2,1,0:T(8,128)(2,1)} custom-call(f32[1,4096]{1,0:T(1,128)} %axial_hbm.1, f32[1,4096]{1,0:T(1,128)} %angle_hbm.1, f32[1,4096]{1,0:T(1,128)} %area_hbm.1, bf16[1,64,256]{2,1,0:T(8,128)(2,1)} %inc_hbm.1, s32[1,2,2,32]{3,2,1,0:T(2,128)} %lit_hbm.1, f32[2,32]{1,0:T(2,128)} %end_hbm.1), custom_call_target="tpu_custom_call" | custom-call | tf_op jit(solution)/shard_map/pallas_call | solution.py:414
  38.7 1.4 %copy.8 = bf16[1,64,256]{2,1,0:T(8,128)(2,1)} copy(bf16[1,64,256]{2,1,0:T(8,128)(2,1)} %shard_map.64) | data formatting | bytes 65536

commit v4 on v3

--- a/solution.py
+++ b/solution.py
@@ -229,31 +229,36 @@
             for c, ref in enumerate((axial_hbm, angle_hbm, area_hbm))
         ]
 
-    steps = [n for k in range(1, ring // 2) for n in (k, ring - k)] + [ring // 2]
+    def spread_one(source, sweep, blocks, slot, n):
+        d = d_far if slot == NEAR else d_near
+        pltpu.make_async_remote_copy(
+            src_ref=source.at[pl.ds(pl.multiple_of(2 * half * d, 2 * half), 2 * half), :],
+            dst_ref=blocks.at[slot, part],
+            send_sem=sent.at[sweep, slot], recv_sem=row_recv.at[sweep, slot, place],
+            device_id=(near, in_row(own_base, n)) if slot == NEAR else (far, in_row(other_base, n)),
+            device_id_type=MESH,
+        ).start()
 
     def spread(source, sweep, blocks, slot):
-        d = d_far if slot == NEAR else d_near
-        for n in [*steps[::-1], 0]:
-            pltpu.make_async_remote_copy(
-                src_ref=source.at[pl.ds(pl.multiple_of(2 * half * d, 2 * half), 2 * half), :],
-                dst_ref=blocks.at[slot, part],
-                send_sem=sent.at[sweep, slot], recv_sem=row_recv.at[sweep, slot, n],
-                device_id=(near, in_row(own_base, n)) if slot == NEAR else (far, in_row(other_base, n)),
-                device_id_type=MESH,
-            ).start()
-
-    def hand_across(sweep, blocks, slot, which):
-        for n in which:
-            block = blocks.at[slot, in_row(own_base if slot == NEAR else other_base, ring - n)]
-
-            def copy(recv):
-                return pltpu.make_async_remote_copy(
-                    src_ref=block, dst_ref=block, send_sem=sent.at[sweep, slot], recv_sem=recv,
-                    device_id=(seg, across), device_id_type=MESH,
-                )
-
-            copy(row_recv.at[sweep, slot, n]).wait_recv()
-            copy(side_recv.at[sweep, slot]).start()
+        for n in [k for m in range(ring // 2, 0, -1) for k in sorted({m, ring - m})] + [0]:
+            spread_one(source, sweep, blocks, slot, n)
+
+    quad = ring // 2
+    own_quad = place // quad
+
+    def hand_across(sweep, blocks, slot, later):
+        start = quad * (1 - own_quad if later else own_quad)
+        base = (own_base if slot == NEAR else other_base) + start
+
+        def copy(ref, recv):
+            return pltpu.make_async_remote_copy(
+                src_ref=ref, dst_ref=ref, send_sem=sent.at[sweep, slot], recv_sem=recv,
+                device_id=(seg, across), device_id_type=MESH,
+            )
+
+        for n in range(quad):
+            copy(blocks.at[slot, base + n], row_recv.at[sweep, slot, start + n]).wait_recv()
+        copy(blocks.at[slot, pl.ds(base, quad)], side_recv.at[sweep, slot]).start()
 
     def whole(sweep, blocks, slot, count):
         some = blocks.at[slot, pl.ds(0, count)]
@@ -278,7 +283,6 @@
     def _():
         for copy in far_geo:
             copy.start()
-        spread(inc_hbm.at[0], 0, cur1, FAR)
 
     for load in loads:
         load.wait()
@@ -290,7 +294,6 @@
 
     buffers = ((q0, soft0), (q1, soft1))
     near_feat, far_feat = tfeat.at[d_near], tfeat.at[d_far]
-    early, late = [0, *steps[:4]], steps[4:]
     pairs = tiles // 2
 
     for copy in near_geo:
@@ -298,15 +301,21 @@
     source_features(geo, NEAR, d_near, lit, sfeat, patches)
 
     def beside_near(k, part_of):
-        if part_of:
-            return
-
-        @pl.when(k == pairs // 2)
+        @pl.when(jnp.logical_and(has_far, k < ring // 2))
         def _():
-            hand_across(0, cur1, NEAR, early)
+            spread_one(inc_hbm.at[0], 0, cur1, FAR, ring // 2 + 2 * k + part_of)
+
+        if part_of == 0:
+
+            @pl.when(k == 4)
+            def _():
+                hand_across(0, cur1, NEAR, False)
+
+            @pl.when(k == 6)
+            def _():
+                hand_across(0, cur1, NEAR, True)
 
     build_table(near_feat, sfeat, NEAR, buffers, near_table, tiles, 0, pairs, beside_near)
-    hand_across(0, cur1, NEAR, late)
 
     first = (column(end[0:1, :], 0, half), column(end[0:1, :], half, half))
     last = (column(end[1:2, :], 0, half), column(end[1:2, :], half, half))
@@ -326,7 +335,7 @@
 
             @pl.when(jnp.logical_and(has_far, k == 1))
             def _():
-                hand_across(0, cur1, FAR, early)
+                hand_across(0, cur1, FAR, False)
 
             @pl.when(k == pairs // 4)
             def _():
@@ -345,10 +354,14 @@
 
     @if_far
     def _():
-        spread(state, 1, cur2, FAR)
-        hand_across(0, cur1, FAR, late)
-
-    build_table(far_feat, sfeat, FAR, buffers, far_table, tiles, pairs // 2, pairs, lambda k, part_of: None)
+        hand_across(0, cur1, FAR, True)
+
+    def beside_rest(k, part_of):
+        @if_far
+        def _():
+            spread_one(state, 1, cur2, FAR, ring // 2 + 2 * (k - pairs // 2) + part_of)
+
+    build_table(far_feat, sfeat, FAR, buffers, far_table, tiles, pairs // 2, pairs, beside_rest)
 
     def far_result(coupled, previous):
         mirrored = reflect(mirror, previous[rows(d_near), :].astype(f32), half)
@@ -366,15 +379,15 @@
 
     @if_far
     def _():
-        hand_across(1, cur2, FAR, early)
-
-    hand_across(1, cur2, NEAR, early)
-
-    @if_far
-    def _():
-        hand_across(1, cur2, FAR, late)
-
-    hand_across(1, cur2, NEAR, late)
+        hand_across(1, cur2, FAR, False)
+
+    hand_across(1, cur2, NEAR, False)
+
+    @if_far
+    def _():
+        hand_across(1, cur2, FAR, True)
+
+    hand_across(1, cur2, NEAR, True)
 
     near_coupled = couple(cur2, NEAR, near_table, own_base, ring, half)
     far_coupled = couple(cur2, FAR, far_table, other_base, ring, half)

time: 40.3 us -> 39.1 us (0.970)
  the two profiles are of different devices: /device:TPU:196 before, /device:TPU:198 now
where the time goes in v4:
time: 39.1 us; the launch traced here: 38.8 us
  Pallas kernels  37.4 us (96%)
  local copies, waits for them, and re-layouts  1.38 us (4%)
    pallas_call x1, Pallas kernels, on_device(): pl.pallas_call(functools.partial(sweep_kernel, segs, parts), out_shape=ja...  37.4 us
    unnamed x1, local copies, waits for them, and re-layouts  1.38 us

profile of v4, /device:TPU:198, one launch (start us, length us, event | category | flops | bytes accessed | tf_op | source)
XLA Modules:
  0.0 38.8 jit_solution(7962501040857300675)
XLA Ops:
  0.0 37.4 %shard_map.64 = bf16[1,64,256]{2,1,0:T(8,128)(2,1)} custom-call(f32[1,4096]{1,0:T(1,128)} %axial_hbm.1, f32[1,4096]{1,0:T(1,128)} %angle_hbm.1, f32[1,4096]{1,0:T(1,128)} %area_hbm.1, bf16[1,64,256]{2,1,0:T(8,128)(2,1)} %inc_hbm.1, s32[1,2,2,32]{3,2,1,0:T(2,128)} %lit_hbm.1, f32[2,32]{1,0:T(2,128)} %end_hbm.1), custom_call_target="tpu_custom_call" | custom-call | tf_op jit(solution)/shard_map/pallas_call | solution.py:427
  37.4 1.4 %copy.8 = bf16[1,64,256]{2,1,0:T(8,128)(2,1)} copy(bf16[1,64,256]{2,1,0:T(8,128)(2,1)} %shard_map.64) | data formatting | bytes 65536

commit v5 on v4

--- a/solution.py
+++ b/solution.py
@@ -258,18 +258,21 @@
 
         for n in range(quad):
             copy(blocks.at[slot, base + n], row_recv.at[sweep, slot, start + n]).wait_recv()
-        copy(blocks.at[slot, pl.ds(base, quad)], side_recv.at[sweep, slot]).start()
-
-    def whole(sweep, blocks, slot, count):
+        copy(blocks.at[slot, pl.ds(base, quad)], side_recv.at[sweep, slot, int(later)]).start()
+
+    def whole(sweep, blocks, slot, count, later=False):
         some = blocks.at[slot, pl.ds(0, count)]
         return pltpu.make_async_remote_copy(
             src_ref=some, dst_ref=some,
-            send_sem=sent.at[sweep, slot], recv_sem=side_recv.at[sweep, slot],
+            send_sem=sent.at[sweep, slot], recv_sem=side_recv.at[sweep, slot, int(later)],
             device_id=(seg, across), device_id_type=MESH,
         )
 
-    def handed_here(sweep, blocks, slot):
-        whole(sweep, blocks, slot, ring).wait_recv()
+    def handed_here(sweep, blocks, slot, later):
+        whole(sweep, blocks, slot, quad, later).wait_recv()
+
+    def half_row(base, later):
+        return base + quad * (1 - own_quad if later else own_quad)
 
     def if_far(act):
         pl.when(has_far)(act)
@@ -339,7 +342,8 @@
 
             @pl.when(k == pairs // 4)
             def _():
-                handed_here(0, cur1, NEAR)
+                handed_here(0, cur1, NEAR, False)
+                handed_here(0, cur1, NEAR, True)
 
         tile = jnp.where(k < pairs // 4, own_base, other_base - ring) + 4 * k + 2 * part_of
         for n in (0, 1):
@@ -371,7 +375,8 @@
 
     @if_far
     def _():
-        handed_here(0, cur1, FAR)
+        handed_here(0, cur1, FAR, False)
+        handed_here(0, cur1, FAR, True)
 
     coupled += couple(cur1, FAR, far_table, own_base, ring, half)
     state[rows(d_far), :] = far_result(coupled, inc)
@@ -380,27 +385,24 @@
     @if_far
     def _():
         hand_across(1, cur2, FAR, False)
-
+        hand_across(1, cur2, FAR, True)
+
+    far_coupled = couple(cur2, FAR, far_table, other_base, ring, half)
     hand_across(1, cur2, NEAR, False)
-
-    @if_far
-    def _():
-        hand_across(1, cur2, FAR, True)
-
     hand_across(1, cur2, NEAR, True)
-
     near_coupled = couple(cur2, NEAR, near_table, own_base, ring, half)
-    far_coupled = couple(cur2, FAR, far_table, other_base, ring, half)
-    handed_here(1, cur2, NEAR)
-    near_coupled += couple(cur2, NEAR, near_table, other_base, ring, half)
-    out_ref[0, rows(d_near), :] = (inc[rows(d_near), :].astype(f32) + near_coupled).astype(bf16)
-
-    @if_far
-    def _():
-        handed_here(1, cur2, FAR)
+
+    @if_far
+    def _():
+        handed_here(1, cur2, FAR, False)
+        handed_here(1, cur2, FAR, True)
 
     far_coupled += couple(cur2, FAR, far_table, own_base, ring, half)
     out_ref[0, rows(d_far), :] = far_result(far_coupled, state)
+    for later in (False, True):
+        handed_here(1, cur2, NEAR, later)
+        near_coupled += couple(cur2, NEAR, near_table, half_row(other_base, later), quad, half)
+    out_ref[0, rows(d_near), :] = (inc[rows(d_near), :].astype(f32) + near_coupled).astype(bf16)
 
     for copy in near_geo:
         copy.wait_send()
@@ -444,7 +446,7 @@
             pltpu.SemaphoreType.DMA((2, 3)),
             pltpu.SemaphoreType.DMA((2, 2)),
             pltpu.SemaphoreType.DMA((2, 2, parts // 2)),
-            pltpu.SemaphoreType.DMA((2, 2)),
+            pltpu.SemaphoreType.DMA((2, 2, 2)),
         ],
         compiler_params=pltpu.CompilerParams(
             collective_id=0, has_side_effects=True, vmem_limit_bytes=56 << 20

time: 39.1 us -> 37.2 us (0.951)
  the two profiles are of different devices: /device:TPU:198 before, /device:TPU:196 now
where the time goes in v5:
time: 37.2 us; the launch traced here: 37 us
  Pallas kernels  35.6 us (96%)
  local copies, waits for them, and re-layouts  1.38 us (4%)
    pallas_call x1, Pallas kernels, on_device(): pl.pallas_call(functools.partial(sweep_kernel, segs, parts), out_shape=ja...  35.6 us
    unnamed x1, local copies, waits for them, and re-layouts  1.38 us

profile of v5, /device:TPU:196, one launch (start us, length us, event | category | flops | bytes accessed | tf_op | source)
XLA Modules:
  0.0 37.0 jit_solution(16946578602051970879)
XLA Ops:
  0.0 35.6 %shard_map.64 = bf16[1,64,256]{2,1,0:T(8,128)(2,1)} custom-call(f32[1,4096]{1,0:T(1,128)} %axial_hbm.1, f32[1,4096]{1,0:T(1,128)} %angle_hbm.1, f32[1,4096]{1,0:T(1,128)} %area_hbm.1, bf16[1,64,256]{2,1,0:T(8,128)(2,1)} %inc_hbm.1, s32[1,2,2,32]{3,2,1,0:T(2,128)} %lit_hbm.1, f32[2,32]{1,0:T(2,128)} %end_hbm.1), custom_call_target="tpu_custom_call" | custom-call | tf_op jit(solution)/shard_map/pallas_call | solution.py:429
  35.6 1.4 %copy.8 = bf16[1,64,256]{2,1,0:T(8,128)(2,1)} copy(bf16[1,64,256]{2,1,0:T(8,128)(2,1)} %shard_map.64) | data formatting | bytes 65536

commit v6 on v5

--- a/solution.py
+++ b/solution.py
@@ -256,9 +256,12 @@
                 device_id=(seg, across), device_id_type=MESH,
             )
 
+        count = 1 if sweep == 1 else quad
         for n in range(quad):
             copy(blocks.at[slot, base + n], row_recv.at[sweep, slot, start + n]).wait_recv()
-        copy(blocks.at[slot, pl.ds(base, quad)], side_recv.at[sweep, slot, int(later)]).start()
+            if (n + 1) % count == 0:
+                some = blocks.at[slot, pl.ds(base + n + 1 - count, count)]
+                copy(some, side_recv.at[sweep, slot, int(later)]).start()
 
     def whole(sweep, blocks, slot, count, later=False):
         some = blocks.at[slot, pl.ds(0, count)]

time: 37.2 us -> 36.8 us (0.989)
  the two profiles are of different devices: /device:TPU:196 before, /device:TPU:195 now
where the time goes in v6:
time: 36.8 us; the launch traced here: 36.5 us
  Pallas kernels  35.2 us (96%)
  local copies, waits for them, and re-layouts  1.38 us (4%)
    pallas_call x1, Pallas kernels, on_device(): pl.pallas_call(functools.partial(sweep_kernel, segs, parts), out_shape=ja...  35.2 us
    unnamed x1, local copies, waits for them, and re-layouts  1.38 us

profile of v6, /device:TPU:195, one launch (start us, length us, event | category | flops | bytes accessed | tf_op | source)
XLA Modules:
  0.0 36.5 jit_solution(1448672557711148673)
XLA Ops:
  0.0 35.2 %shard_map.64 = bf16[1,64,256]{2,1,0:T(8,128)(2,1)} custom-call(f32[1,4096]{1,0:T(1,128)} %axial_hbm.1, f32[1,4096]{1,0:T(1,128)} %angle_hbm.1, f32[1,4096]{1,0:T(1,128)} %area_hbm.1, bf16[1,64,256]{2,1,0:T(8,128)(2,1)} %inc_hbm.1, s32[1,2,2,32]{3,2,1,0:T(2,128)} %lit_hbm.1, f32[2,32]{1,0:T(2,128)} %end_hbm.1), custom_call_target="tpu_custom_call" | custom-call | tf_op jit(solution)/shard_map/pallas_call | solution.py:432
  35.2 1.4 %copy.8 = bf16[1,64,256]{2,1,0:T(8,128)(2,1)} copy(bf16[1,64,256]{2,1,0:T(8,128)(2,1)} %shard_map.64) | data formatting | bytes 65536
